TPU v7x, 512 devices: a whole 4x8x8 slice. The times are simulated.
512 devices in a mesh: dp: 32 (over y_lo, x, core), shard: 16 (over y_hi, z).
Axes of the slice: x: 4, y: 8 (y_hi: 2, y_lo: 4; y = y_hi * 4 + y_lo), z: 8, core: 2. Of those that a mesh axis runs over, the one named last changes fastest.
Arguments:
- residual_in: bfloat16 [24576, 4096], P(('dp', 'shard')), may hold values from -24 to 24
- conv_out: bfloat16 [24576, 8192], P('dp', 'shard'), may hold values from -6 to 6
- b_proj: bfloat16 [24576, 512], P('dp'), may hold values from -2 to 2
- c_proj: bfloat16 [24576, 512], P('dp'), may hold values from -2 to 2
- grad_out: bfloat16 [24576, 8192], P('dp', 'shard'), may hold values from -6 to 6
- doc_starts: int32 [24576], P('dp'), may hold values from 0 to 1, as said below
- dest_plan: int32 [512], P('dp'), may hold values from 0 to 31, as said below
- dt_weight: bfloat16 [4096, 128], P('shard'), may hold values from -0.09375 to 0.09375
- dt_bias: float32 [128], replicated, may hold values from -3 to 0
- decay_rate: float32 [128], replicated, may hold values from 0.02 to 0.5
- skip_gain: float32 [128], replicated, may hold values from 0.5 to 1.5
Outputs:
- conv_grad: bfloat16 [24576, 8192], P('dp', 'shard')
- dt_weight_grad: float32 [4096, 128], P('shard')
Inputs may be any that keep to these rules, and one draw needn't show every extreme that they name: `doc_starts`: the first token of every aligned block of 48 tokens is 1; a 1 begins a document, which runs up to the next 1. `dest_plan`: the 16 blocks of one dp index go to 16 different dp indices, and every dp index receives exactly one block in each of its 16 block positions.
All inputs are finite; a program needn't handle non-finite values.
Results may differ from a plain program's by a relative error of at most 0.0043.
Values may be sent and summed in bfloat16 or wider, within the bound.
A program may use at most 64 MiB of HBM per device.

v0:
```python
import jax
import jax.numpy as jnp
from jax import lax
from jax.sharding import PartitionSpec as P

N = 128
G = 4


def group_grads(pre, values, b_rows, c_rows, starts, upstream, bias, rate, gain, block_len):
    rows, heads = pre.shape
    width = values.shape[1] // heads
    count = rows // block_len
    gate_in = pre + bias[None, :]
    step_size = jax.nn.softplus(gate_in)
    log_decay = -step_size * rate[None, :]
    level = jnp.cumsum(log_decay.reshape(count, block_len, heads), axis=1).transpose(0, 2, 1)
    segment = jnp.cumsum(starts.reshape(count, block_len), axis=1)
    position = jnp.arange(block_len)
    causal = position[:, None] >= position[None, :]
    allowed = (segment[:, :, None] == segment[:, None, :]) & causal[None]
    c_blocks = c_rows.reshape(count, block_len, -1)
    b_blocks = b_rows.reshape(count, block_len, -1)
    score = jnp.einsum("cin,cjn->cij", c_blocks, b_blocks, preferred_element_type=jnp.float32)
    steps_t = step_size.reshape(count, block_len, heads).transpose(0, 2, 1)
    spread = level[:, :, :, None] - level[:, :, None, :]
    mask = allowed[:, None]
    decay = jnp.where(mask, jnp.exp(jnp.where(mask, spread, 0.0)), 0.0)
    mixing = (score[:, None] * decay * steps_t[:, :, None, :]).astype(jnp.bfloat16)
    vals = values.reshape(count, block_len, heads, width)
    ups = upstream.reshape(count, block_len, heads, width)
    grad_mixing = jnp.einsum("cihp,cjhp->chij", ups, vals, preferred_element_type=jnp.float32)
    grad_values = jnp.einsum("chij,cihp->cjhp", mixing, ups, preferred_element_type=jnp.float32)
    weighted = grad_mixing * score[:, None] * decay
    grad_step = jnp.sum(weighted, axis=2)
    flow = weighted * steps_t[:, :, None, :]
    grad_level = jnp.sum(flow, axis=3) - jnp.sum(flow, axis=2)
    grad_log = jnp.flip(jnp.cumsum(jnp.flip(grad_level, 2), axis=2), 2)
    combined = grad_step - rate[None, :, None] * grad_log
    grad_pre = combined.transpose(0, 2, 1).reshape(rows, heads) * jax.nn.sigmoid(gate_in)
    grad_conv = grad_values.reshape(rows, heads * width) + jnp.repeat(gain, width)[
        None, :
    ] * upstream.astype(jnp.float32)
    return (grad_conv.astype(jnp.bfloat16), grad_pre)


def project(tokens, dt_weight):
    return jnp.dot(
        tokens,
        lax.all_gather(dt_weight, "shard", axis=0, tiled=True),
        preferred_element_type=jnp.float32,
    )


def on_device(
    residual_in,
    conv_out,
    b_proj,
    c_proj,
    grad_out,
    doc_starts,
    dest_plan,
    dt_weight,
    dt_bias,
    decay_rate,
    skip_gain,
):
    n_data = lax.axis_size("dp")
    n_shard = lax.axis_size("shard")
    block_len = residual_in.shape[0]
    rows = conv_out.shape[0]
    block_count = rows // block_len
    head_total = dt_bias.shape[0]
    heads_here = head_total // n_shard
    per_group = head_total // G
    first_head = lax.axis_index("shard") * heads_here
    group = first_head // per_group
    b_group = lax.dynamic_slice_in_dim(b_proj, group * N, N, 1)
    c_group = lax.dynamic_slice_in_dim(c_proj, group * N, N, 1)
    bias_here = lax.dynamic_slice_in_dim(dt_bias, first_head, heads_here, 0)
    rate_here = lax.dynamic_slice_in_dim(decay_rate, first_head, heads_here, 0)
    gain_here = lax.dynamic_slice_in_dim(skip_gain, first_head, heads_here, 0)
    local_pre = project(residual_in, dt_weight)
    pre_here = lax.all_to_all(local_pre, "shard", split_axis=1, concat_axis=0, tiled=True)
    slot_ids = jnp.arange(1, block_count + 1, dtype=jnp.int32)
    destinations = jnp.arange(n_data, dtype=jnp.int32)
    chosen = dest_plan[:, None] == destinations[None, :]
    labels = jnp.sum(jnp.where(chosen, slot_ids[:, None], 0), axis=0)
    arrived = lax.all_to_all(
        labels.reshape(n_data, 1), "dp", split_axis=0, concat_axis=0, tiled=True
    )[:, 0]
    sources = jnp.sum(
        jnp.where(arrived[None, :] == slot_ids[:, None], destinations[None, :], 0), axis=1
    )
    grad_conv, grad_pre = group_grads(
        pre_here,
        conv_out,
        b_group,
        c_group,
        doc_starts,
        grad_out,
        bias_here,
        rate_here,
        gain_here,
        block_len,
    )
    blocks = grad_conv.reshape((block_count, block_len) + grad_conv.shape[1:])
    picked = jnp.take(blocks, jnp.maximum(labels - 1, 0), axis=0)
    keep = (labels > 0).reshape((n_data,) + (1,) * (blocks.ndim - 1))
    returned = lax.all_to_all(
        jnp.where(keep, picked, jnp.zeros_like(picked)),
        "dp",
        split_axis=0,
        concat_axis=0,
        tiled=True,
    )
    picked = jnp.take(returned, sources, axis=0)
    conv_grad = picked.reshape((rows,) + returned.shape[2:])
    grad_pre_b = grad_pre.astype(jnp.bfloat16)
    grad_rows = lax.all_to_all(grad_pre_b, "shard", split_axis=0, concat_axis=1, tiled=True)
    partial_grad = jnp.einsum(
        "rd,rh->dh", residual_in, grad_rows, preferred_element_type=jnp.float32
    )
    scale = float(rows * n_data) ** (-0.5)
    shard_part = lax.psum_scatter(partial_grad, "shard", scatter_dimension=0, tiled=True)
    summed = lax.psum(shard_part, "dp")
    return (conv_grad, summed * scale)


def solution(mesh):
    placed = (
        P(("dp", "shard"), None),
        P("dp", "shard"),
        P("dp", None),
        P("dp", None),
        P("dp", "shard"),
        P("dp"),
        P("dp"),
        P("shard", None),
        P(),
        P(),
        P(),
    )
    return jax.shard_map(
        on_device,
        mesh=mesh,
        in_specs=placed,
        out_specs=(P("dp", "shard"), P("shard", None)),
        check_vma=False,
    )
```

profile of v0, /device:TPU:1, one launch (start us, length us, event | category | flops | bytes accessed | tf_op | source)
XLA Modules:
  0.0 667.2 jit_solution(10398825576780462844)
XLA Ops:
  9.0 1.1 constant_dynamic-slice_fusion
  10.9 1.0 fusion.29
  11.9 90.0 %all-gather.2.cloned.1.call-done = bf16[4096,128]{1,0:T(8,128)(2,1)} async-done(((bf16[256,128]{1,0:T(8,128)(2,1)}), bf16[4096,128]{1,0:T(8,128)(2,1)}) %all-gather.2.cloned.1.call-update) | async-done | bytes 1048592 | tf_op jit(solution)/shard_map/all_gather | solution.py:50
  102.0 1.7 fusion.26
  104.4 4.7 all-to-all-start.1
  110.2 2.5 reshape.137
  112.7 7.8 %all-to-all-done.1 = f32[16,1,384]{2,1,0:T(1,128)} async-done(((f32[16,1,384]{2,1,0:T(1,128)}), f32[16,1,384]{2,1,0:T(1,128)}, u32[]{:S(2)}, u32[]{:S(2)}) %all-to-all-start.1) | async-done | bytes 24608 | tf_op jit(solution)/shard_map/all_to_all | solution.py:84
  120.9 2.0 reduce.1
  122.9 1.4 reshape.157
  124.4 1.6 compare_select_fusion
  125.9 1.6 fusion.10
  127.5 1.8 copy.56
  129.3 1.8 reduce-window_bitcast_fusion
  131.1 1.8 copy.57
  132.9 4.5 multiply_reduce_fusion
  137.4 3.3 reduce_window_sum.35
  140.8 1.0 fusion.28
  142.5 3.7 all-to-all-start.3
  147.4 10.0 %all-to-all-done.3 = bf16[16,2,192]{2,1,0:T(2,128)(2,1)S(1)} async-done(((bf16[16,2,192]{2,1,0:T(2,128)(2,1)}), bf16[16,2,192]{2,1,0:T(2,128)(2,1)S(1)}, u32[]{:S(2)}, u32[]{:S(2)}) %all-to-all-start.3) | async-done | bytes 12320 | tf_op jit(solution)/shard_map/all_to_all | solution.py:120
  157.4 16.0 %all-to-all-start = ((s32[32,1,1]{2,1,0:T(1,128)}), s32[32,1,1]{2,1,0:T(1,128)S(1)}, u32[]{:S(2)}, u32[]{:S(2)}) async-start(s32[32,1,1]{2,1,0:T(1,128)} %copy.54), calls=%async_computation | async-start | bytes 32768 | tf_op jit(solution)/shard_map/all_to_all | solution.py:89
  173.5 1.8 convolution_bitcast_fusion
  177.4 2.8 convolution_bitcast_fusion.1
  180.2 1.0 copy.61
  181.2 1.7 reshape.135
  182.9 1.9 add_convert_fusion
  185.6 1.4 select_select_fusion
  187.1 7.7 %all-to-all-start.2 = ((bf16[32,48,512]{2,1,0:T(8,128)(2,1)}), bf16[32,48,512]{2,1,0:T(8,128)(2,1)S(1)}, u32[]{:S(2)}, u32[]{:S(2)}) async-start(bf16[32,48,512]{2,1,0:T(8,128)(2,1)} %select_select_fusion), calls=%async_computation.2 | async-start | bytes 3145728 | tf_op jit(solution)/shard_map/all_to_all | solution.py:110
  195.9 38.6 %all-to-all-done.2 = bf16[32,48,512]{2,1,0:T(8,128)(2,1)S(1)} async-done(((bf16[32,48,512]{2,1,0:T(8,128)(2,1)}), bf16[32,48,512]{2,1,0:T(8,128)(2,1)S(1)}, u32[]{:S(2)}, u32[]{:S(2)}) %all-to-all-start.2) | async-done | bytes 1572896 | tf_op jit(solution)/shard_map/all_to_all | solution.py:110
  235.1 163.5 %reduce-scatter.2.cloned.1.call-done = f32[256,128]{0,1:T(8,128)} async-done(((f32[4096,128]{0,1:T(8,128)}), f32[256,128]{0,1:T(8,128)}) %reduce-scatter.2.cloned.1.call-update) | async-done | bytes 131088 | tf_op jit(solution)/shard_map/reduce_scatter | solution.py:125
  398.7 1.1 bitcast_select_fusion
  399.7 259.2 %all-reduce.2.cloned.1.call-done = f32[256,128]{0,1:T(8,128)} async-done(((f32[256,128]{0,1:T(8,128)}), f32[256,128]{0,1:T(8,128)}) %all-reduce.2.cloned.1.call-update) | async-done | bytes 131088 | tf_op jit(solution)/shard_map/psum | solution.py:126
  659.0 0.9 broadcast_multiply_fusion
  (72 shorter events, 12.4 us)
Async XLA Ops:
  7.2 94.8 %copy-start = (bf16[48,4096]{1,0:T(8,128)(2,1)S(1)}, bf16[48,4096]{1,0:T(8,128)(2,1)}, u32[]{:S(2)}) copy-start(bf16[48,4096]{1,0:T(8,128)(2,1)} %param.11) | copy-start | bytes 1179652
  7.2 94.8 %all-gather.2.cloned.1.call-start = ((), (), s32[]{:S(2)}) async-start(), calls=%async_computation.5 | async-start | bytes 1114112 | tf_op jit(solution)/shard_map/all_gather | solution.py:50
  8.9 100.2 %copy-start.14 = (s32[16]{0:T(128)}, s32[16]{0:T(128)S(1)}, u32[]{:S(2)}) copy-start(s32[16]{0:T(128)S(1)} %iota_add_fusion) | copy-start | bytes 196
  8.9 100.2 %copy-start.10 = (s32[16]{0:T(128)S(1)}, s32[16]{0:T(128)}, u32[]{:S(2)}) copy-start(s32[16]{0:T(128)} %param.17) | copy-start | bytes 196
  8.9 100.3 %copy-start.11 = (f32[128]{0:T(128)S(1)}, f32[128]{0:T(128)}, u32[]{:S(2)}) copy-start(f32[128]{0:T(128)} %param.19) | copy-start | bytes 1540
  8.9 100.4 %copy-start.12 = (f32[128]{0:T(128)S(1)}, f32[128]{0:T(128)}, u32[]{:S(2)}) copy-start(f32[128]{0:T(128)} %param.20) | copy-start | bytes 1540
  9.0 100.4 %copy-start.1 = (bf16[768,512]{1,0:T(8,128)(2,1)S(1)}, bf16[768,512]{1,0:T(8,128)(2,1)}, u32[]{:S(2)}) copy-start(bf16[768,512]{1,0:T(8,128)(2,1)} %param.15) | copy-start | bytes 2359300
  104.4 16.0 %all-to-all-start.1 = ((f32[16,1,384]{2,1,0:T(1,128)}), f32[16,1,384]{2,1,0:T(1,128)}, u32[]{:S(2)}, u32[]{:S(2)}) async-start(f32[16,1,384]{2,1,0:T(1,128)} %reshape.156), calls=%async_computation.1 | async-start | bytes 49152 | tf_op jit(solution)/shard_map/all_to_all | solution.py:84
  109.2 37.5 %copy-start.8 = (s32[32]{0:T(128)}, s32[32]{0:T(128)S(1)}, u32[]{:S(2)}) copy-start(s32[32]{0:T(128)S(1)} %select_reduce_fusion.1) | copy-start | bytes 388
  142.5 14.9 %all-to-all-start.3 = ((bf16[16,2,192]{2,1,0:T(2,128)(2,1)}), bf16[16,2,192]{2,1,0:T(2,128)(2,1)S(1)}, u32[]{:S(2)}, u32[]{:S(2)}) async-start(bf16[16,2,192]{2,1,0:T(2,128)(2,1)} %reshape.158), calls=%async_computation.3 | async-start | bytes 32768 | tf_op jit(solution)/shard_map/all_to_all | solution.py:120
  157.4 29.7 %all-to-all-start = ((s32[32,1,1]{2,1,0:T(1,128)}), s32[32,1,1]{2,1,0:T(1,128)S(1)}, u32[]{:S(2)}, u32[]{:S(2)}) async-start(s32[32,1,1]{2,1,0:T(1,128)} %copy.54), calls=%async_computation | async-start | bytes 32768 | tf_op jit(solution)/shard_map/all_to_all | solution.py:89
  173.4 225.3 %reduce-scatter.2.cloned.1.call-start = ((), (), s32[]{:S(2)}) async-start(), calls=%async_computation.6 | async-start | bytes 2228224 | tf_op jit(solution)/shard_map/reduce_scatter | solution.py:125
  175.3 0.7 copy-start.9
  175.3 0.7 copy-start.13
  175.3 2.1 copy-start.2
  175.3 2.1 copy-start.3
  175.3 2.1 copy-start.4
  175.3 2.1 copy-start.5
  184.8 0.8 copy-start.6
  184.8 0.8 copy-start.7
  187.1 8.5 %copy-start.15 = (s32[16]{0:T(128)S(1)}, s32[16]{0:T(128)}, u32[]{:S(2)}) copy-start(s32[16]{0:T(128)} %copy-done.14) | copy-start | bytes 196
  187.1 47.4 %all-to-all-start.2 = ((bf16[32,48,512]{2,1,0:T(8,128)(2,1)}), bf16[32,48,512]{2,1,0:T(8,128)(2,1)S(1)}, u32[]{:S(2)}, u32[]{:S(2)}) async-start(bf16[32,48,512]{2,1,0:T(8,128)(2,1)} %select_select_fusion), calls=%async_computation.2 | async-start | bytes 3145728 | tf_op jit(solution)/shard_map/all_to_all | solution.py:110
  194.8 464.2 %all-reduce.2.cloned.1.call-start = ((), (), s32[]{:S(2)}) async-start(), calls=%async_computation.7 | async-start | bytes 262144 | tf_op jit(solution)/shard_map/psum | solution.py:126
Sparse Core Ops, SparseCore 0:
  11.2 90.7 all-gather.1
  178.7 219.9 reduce-scatter.1
  401.6 257.3 all-reduce.1
where the time goes:
time: 668 us; the launch traced here: 667 us
  waiting for transfers between devices  570 us (85%)
  starting transfers between devices  32.2 us (5%)
  local copies, waits for them, and re-layouts  19.7 us (3%)
  other arithmetic  19.6 us (3%)
  between operations  14 us (2%)
  matrix products  11.8 us (2%)
    psum x1, waiting for transfers between devices, on_device(): summed = lax.psum(shard_part, 'dp')  259 us
    reduce_scatter x1, waiting for transfers between devices, on_device(): lax.psum_scatter(partial_grad, 'shard', scatter_dimension=0, tiled=True)  164 us
    all_gather x1, waiting for transfers between devices, project(): lax.all_gather(dt_weight, 'shard', axis=0, tiled=True)  90 us
    all_to_all x1, waiting for transfers between devices, on_device(): lax.all_to_all(jnp.where(keep, picked, jnp.zeros_like(picked)), 'dp', spl...  38.6 us
    all_to_all x1, starting transfers between devices, on_device(): lax.all_to_all(labels.reshape(n_data, 1), 'dp', split_axis=0, concat_axis...  16 us
  transfers between devices with their start and end apart: 7, of which 6 were waited for; matrix products, arithmetic and copies ran while one was open for 4% of the time, Pallas kernels for 0%

commit v1 on v0

v1 whole, which is shorter than its diff:
```python
import functools

import jax
import jax.numpy as jnp
from jax import lax
from jax.experimental import pallas as pl
from jax.experimental.pallas import tpu as pltpu
from jax.sharding import PartitionSpec as P

N = 128
G = 4
BLK = 48
LANES = 128
MESH = pl.DeviceIdType.MESH
F32 = jnp.float32
BF16 = jnp.bfloat16
NT = (((1,), (1,)), ((), ()))
NN = (((1,), (0,)), ((), ()))
N_YHI = 2


class Grid:
    def __init__(self, n_dp, n_shard):
        self.n_dp = n_dp
        self.n_z = n_shard // N_YHI
        self.n_core = 2
        rest = n_dp // 2
        self.n_hb = 2 if rest >= 2 else 1
        rest //= self.n_hb
        self.n_x = min(rest, 4)
        self.n_lb = rest // self.n_x
        self.n_y = self.n_hb * self.n_lb

    def here(self):
        dp = lax.axis_index("dp")
        shard = lax.axis_index("shard")
        core = lax.rem(dp, self.n_core)
        x = lax.rem(dp // self.n_core, self.n_x)
        y = dp // (self.n_core * self.n_x)
        return dp, y, x, core, shard // self.n_z, lax.rem(shard, self.n_z)

    def dp_of(self, y, x, core):
        return (y * self.n_x + x) * self.n_core + core

    def partner(self, s):
        _, y, x, core, _, _ = self.here()
        mc = self.n_core - 1 - s % self.n_core
        mx = self.n_x - 1 - (s // self.n_core) % self.n_x
        t = s // (self.n_core * self.n_x)
        hb = y // self.n_lb
        lb = y % self.n_lb
        hb2 = (hb + self.n_hb - 1 + t // self.n_lb) % self.n_hb
        lb2 = (lb + self.n_lb - 1 + t % self.n_lb) % self.n_lb
        if self.n_lb == 1:
            lb2 = lb
        return self.dp_of(hb2 * self.n_lb + lb2, (x + mx) % self.n_x, (core + mc) % self.n_core)

    def source(self, s):
        _, y, x, core, _, _ = self.here()
        mc = self.n_core - 1 - s % self.n_core
        mx = self.n_x - 1 - (s // self.n_core) % self.n_x
        t = s // (self.n_core * self.n_x)
        hb = y // self.n_lb
        lb = y % self.n_lb
        hb2 = (hb + self.n_hb - 1 + t // self.n_lb) % self.n_hb
        lb2 = (lb + self.n_lb - 1 + t % self.n_lb) % self.n_lb
        if self.n_lb == 1:
            lb2 = lb
        return self.dp_of(hb2 * self.n_lb + lb2, (x + self.n_x - mx) % self.n_x, (core + mc) % self.n_core)


def remote(src, dst, send, recv, device):
    return pltpu.make_async_remote_copy(
        src_ref=src, dst_ref=dst, send_sem=send, recv_sem=recv, device_id=device, device_id_type=MESH
    )


def spread_lanes(whole, index):
    width = whole.shape[1]
    low = index * BLK
    if width % LANES:
        return jnp.pad(whole[:, low : low + BLK], ((0, 0), (0, LANES - BLK)))
    tile, off = low // LANES, low % LANES
    first = whole[:, tile * LANES : (tile + 1) * LANES]
    if off == 0:
        return first
    first = pltpu.roll(first, LANES - off, 1)
    if off + BLK <= LANES:
        return first
    second = pltpu.roll(whole[:, (tile + 1) * LANES : (tile + 2) * LANES], LANES - off, 1)
    lane = lax.broadcasted_iota(jnp.int32, first.shape, 1)
    return jnp.where(lane < LANES - off, first, second)


def gather_lanes(pieces):
    count = len(pieces)
    width = count * BLK
    if width % LANES:
        return jnp.concatenate([p[:, :BLK] for p in pieces], axis=1)
    lane = lax.broadcasted_iota(jnp.int32, (8, LANES), 1)
    tiles = [jnp.zeros((8, LANES), F32) for _ in range(width // LANES)]
    for index, piece in enumerate(pieces):
        low = index * BLK
        tile, off = low // LANES, low % LANES
        moved = pltpu.roll(piece, off, 1) if off else piece
        tiles[tile] = jnp.where((lane >= off) & (lane < off + BLK), moved, tiles[tile])
        if off + BLK > LANES:
            tiles[tile + 1] = jnp.where(lane < off + BLK - LANES, moved, tiles[tile + 1])
    return jnp.concatenate(tiles, axis=1)


def project_kernel(
    grid, x_ref, w_ref, xg_ref, pre_ref, wo_ref, full_ref, part_ref, rs_ref, give_ref, take_ref,
    xs_sem, xr_sem, ws_sem, wr_sem, ps_sem, pr_sem, ss_sem, sr_sem, local_sem,
):
    n_z = grid.n_z
    _, _, _, _, yh, z = grid.here()
    half = n_z * BLK
    feats = w_ref.shape[0]

    def peer(step):
        return {"shard": yh * n_z + (z + step) % n_z}

    across = {"shard": (1 - yh) * n_z + z}
    barrier = pltpu.get_barrier_semaphore()
    for step in range(1, n_z):
        pl.semaphore_signal(barrier, inc=1, device_id=peer(step), device_id_type=MESH)
    pl.semaphore_signal(barrier, inc=1, device_id=across, device_id_type=MESH)

    def columns(side, step):
        owner = (yh if side == 0 else 1 - yh) * n_z + (z + step) % n_z
        return x_ref.at[:, pl.ds(pl.multiple_of(owner * feats, feats), feats)]

    mine = pl.ds(pl.multiple_of(z * BLK, BLK), BLK)
    own = [pltpu.make_async_copy(columns(side, 0), xg_ref.at[side, mine], local_sem.at[side]) for side in range(2)]
    for copy in own:
        copy.start()
    pl.semaphore_wait(barrier, n_z)
    copies = []
    swap = remote(w_ref, wo_ref, ws_sem, wr_sem, across)
    swap.start()
    for step in range(1, n_z):
        for side in range(2):
            copy = remote(
                columns(side, step), xg_ref.at[side, mine],
                xs_sem.at[step, side], xr_sem.at[step, side], peer(step),
            )
            copy.start()
            copies.append(copy)
    w_here = w_ref[...].astype(F32).T.astype(BF16)
    for copy in own:
        copy.wait()
    swap.wait()
    w_other = wo_ref[...].astype(F32).T.astype(BF16)
    for copy in copies:
        copy.wait()
    full_ref[...] = lax.dot_general(w_here, xg_ref[0], NT, preferred_element_type=F32) + lax.dot_general(
        w_other, xg_ref[1], NT, preferred_element_type=F32
    )
    copies = []
    for step in list(range(1, n_z)) + [0]:
        for side in range(2):
            owner = (yh if side == 0 else 1 - yh) * n_z + (z + step) % n_z
            part_ref[step, side * 8 : (side + 1) * 8] = full_ref[pl.ds(pl.multiple_of(owner * 8, 8), 8)]
        if step:
            copy = remote(part_ref.at[step], rs_ref.at[step], ps_sem.at[step], pr_sem.at[step], peer(step))
            copy.start()
            copies.append(copy)
    total = part_ref[0]
    for step, copy in enumerate(copies, 1):
        copy.wait()
        total = total + rs_ref[step]
    give_ref[...] = total[8:]
    swap = remote(give_ref, take_ref, ss_sem, sr_sem, across)
    swap.start()
    for block in range(n_z):
        pre_ref[yh * n_z + block] = spread_lanes(total[:8], block)
    swap.wait()
    other = take_ref[...]
    for block in range(n_z):
        pre_ref[(1 - yh) * n_z + block] = spread_lanes(other, block)


def project(grid, tokens, weight):
    n_z = grid.n_z
    half = n_z * BLK
    feats, heads = weight.shape
    dma = pltpu.SemaphoreType.DMA
    return pl.pallas_call(
        functools.partial(project_kernel, grid),
        out_shape=(
            jax.ShapeDtypeStruct((2, half, feats), BF16),
            jax.ShapeDtypeStruct((2 * n_z, 8, LANES), F32),
        ),
        in_specs=[pl.BlockSpec(memory_space=pl.ANY), pl.BlockSpec(memory_space=pltpu.VMEM)],
        out_specs=[pl.BlockSpec(memory_space=pltpu.VMEM)] * 2,
        scratch_shapes=[
            pltpu.VMEM((feats, heads), BF16),
            pltpu.VMEM((heads, half), F32),
            pltpu.VMEM((n_z, 16, half), F32),
            pltpu.VMEM((n_z, 16, half), F32),
            pltpu.VMEM((8, half), F32),
            pltpu.VMEM((8, half), F32),
            dma((n_z, 2)), dma((n_z, 2)), dma, dma, dma((n_z,)), dma((n_z,)), dma, dma, dma((2,)),
        ],
        compiler_params=pltpu.CompilerParams(
            collective_id=0, has_side_effects=True, vmem_limit_bytes=32 * 1024 * 1024
        ),
        cost_estimate=pl.CostEstimate(flops=10**8, bytes_accessed=2 * 10**6, transcendentals=0),
    )(tokens, weight)


def triangles():
    row = lax.broadcasted_iota(jnp.int32, (LANES, LANES), 0)
    col = lax.broadcasted_iota(jnp.int32, (LANES, LANES), 1)
    same = (row < BLK) == (col < BLK)
    upper = jnp.where(row <= col, 1.0, 0.0).astype(F32)
    ahead = jnp.where((row <= col) & same, 1.0, 0.0).astype(F32)
    behind = jnp.where((row >= col) & same, 1.0, 0.0).astype(F32)
    return upper, ahead, behind


def exact_dot(a, b):
    return lax.dot_general(a, b, NN, preferred_element_type=F32, precision=lax.Precision.HIGHEST)


def split_dot(a, b):
    high = b.astype(BF16)
    low = (b - high.astype(F32)).astype(BF16)
    return lax.dot_general(a, high, NT, preferred_element_type=F32) + lax.dot_general(
        a, low, NT, preferred_element_type=F32
    )


def mixer_pair(first, second, pre_ref, starts_ref, rate, bias, gain, x_ref, go_ref, b_ref, c_ref):
    pair = 2 * BLK
    lane = lax.broadcasted_iota(jnp.int32, (8, LANES), 1)
    pre = jnp.where(lane < BLK, pre_ref[first], pltpu.roll(pre_ref[second], BLK, 1))
    starts = jnp.where(lane < BLK, starts_ref[first], pltpu.roll(starts_ref[second], BLK, 1))
    starts = jnp.where(lane < pair, starts, 1.0)
    gate = jnp.where(lane < pair, pre + bias, 0.0)
    e = jnp.exp(-jnp.abs(gate))
    series = e * (1.0 - e * (0.5 - e * (1.0 / 3.0 - e * (0.25 - e * 0.2))))
    log1p = jnp.where(e < 0.02, series, jnp.log(1.0 + e))
    step = jnp.maximum(gate, 0.0) + log1p
    sig = jnp.where(gate >= 0, 1.0, e) / (1.0 + e)
    ratio = jnp.where((gate < 0) & (e < 1e-6), 1.0, sig / jnp.maximum(step, 1e-20))
    upper, ahead, behind = triangles()
    level = exact_dot(jnp.where(lane < pair, -step * rate, 0.0), ahead)
    segment = lax.dot_general(starts.astype(BF16), upper.astype(BF16), NN, preferred_element_type=F32)
    rows = jnp.concatenate([level, step, segment, jnp.zeros((LANES - 24, LANES), F32)], axis=0)
    cols = rows.T
    ii = lax.broadcasted_iota(jnp.int32, (pair, LANES), 0)
    jj = lax.broadcasted_iota(jnp.int32, (pair, LANES), 1)
    same = cols[:pair, 16:17] == segment[0:1]
    away = jnp.where(same & (jj <= ii), 0.0, -1e30)
    away_t = jnp.where(same & (jj >= ii), 0.0, -1e30)

    def both(ref, low, width):
        return jnp.concatenate([ref[first, :, low : low + width], ref[second, :, low : low + width]], axis=0)

    pad = jnp.zeros((LANES - pair, LANES), BF16)
    b = both(b_ref, 0, N)
    c = both(c_ref, 0, N)
    score = lax.dot_general(c, jnp.concatenate([b, pad], axis=0), NT, preferred_element_type=F32)
    score_t = lax.dot_general(b, jnp.concatenate([c, pad], axis=0), NT, preferred_element_type=F32)
    grads, by_value, by_grad = [], [], []
    low_half = jj < 64
    for duo in range(4):
        mix, mix_t = [], []
        for head in (2 * duo, 2 * duo + 1):
            level_col = cols[:pair, head : head + 1]
            step_col = cols[:pair, 8 + head : 9 + head]
            level_row = level[head : head + 1]
            step_row = step[head : head + 1]
            mix.append((score * jnp.exp(level_col - level_row + away) * step_row).astype(BF16))
            mix_t.append((score_t * jnp.exp(level_row - level_col + away_t) * step_col).astype(BF16))
        x = both(x_ref, duo * LANES, LANES)
        go = both(go_ref, duo * LANES, LANES)
        y = lax.dot_general(
            jnp.concatenate(mix, axis=0), jnp.concatenate([x, pad], axis=0), NN, preferred_element_type=F32
        )
        gv = lax.dot_general(
            jnp.concatenate(mix_t, axis=0), jnp.concatenate([go, pad], axis=0), NN, preferred_element_type=F32
        )
        y = jnp.where(low_half, y[:pair], y[pair:])
        gv = jnp.where(low_half, gv[:pair], gv[pair:])
        go = go.astype(F32)
        grads.append((gv + gain[0:1, duo * LANES : (duo + 1) * LANES] * go).astype(BF16))
        by_value.append(x.astype(F32) * gv)
        by_grad.append(go * y)
    zeros = jnp.zeros((LANES - pair, 4 * LANES), F32)
    head_of = lax.broadcasted_iota(jnp.int32, (8, 4 * LANES), 1) // 64
    pick = jnp.where(head_of == lax.broadcasted_iota(jnp.int32, (8, 4 * LANES), 0), 1.0, 0.0).astype(BF16)
    inflow = split_dot(pick, jnp.concatenate([jnp.concatenate(by_value, axis=1), zeros], axis=0))
    outflow = split_dot(pick, jnp.concatenate([jnp.concatenate(by_grad, axis=1), zeros], axis=0))
    grad_log = exact_dot(outflow - inflow, behind)
    grad_pre = inflow * ratio - rate * grad_log * sig
    return grads, grad_pre


def mixer_kernel(
    grid, scale, n_block,
    plan_ref, pre_ref, starts_ref, consts_ref, gain_ref, x_any, go_any, b_any, c_any, xg_ref,
    recv_ref, dw_ref,
    x_ref, go_ref, b_ref, c_ref, comp_ref, send_ref, gps_ref, half_ref, swap_ref, msg_ref, all_ref, heads_ref,
    xt_ref, d_ref, e1_ref, a1_ref, e2_ref, a2_ref, e3_ref,
    load_sem, es_sem, er_sem, ws_sem, wr_sem, gs_sem, gr_sem, cs_sem, cr_sem, xs_sem, xr_sem, ys_sem, yr_sem,
    fs_sem, fr_sem, hs_sem, hr_sem, ks_sem, kr_sem, own_sem,
):
    n_z, n_x, n_y, n_dp = grid.n_z, grid.n_x, grid.n_y, grid.n_dp
    dp, yy, xx, core, yh, z = grid.here()
    shard = yh * n_z + z
    other = (1 - yh) * n_z + z
    across = {"shard": other}

    def at_z(step):
        return {"shard": yh * n_z + (z + step) % n_z}

    def at_x(step):
        return {"dp": grid.dp_of(yy, (xx + step) % n_x, core)}

    def at_y(side, step):
        place = grid.dp_of((yy + step) % n_y, xx, core)
        return {"dp": place, "shard": shard if side == 0 else other}

    sibling = {"dp": grid.dp_of(yy, xx, 1 - core)}

    barrier = pltpu.get_barrier_semaphore()

    @pl.loop(0, n_dp - 1)
    def _(s):
        pl.semaphore_signal(barrier, inc=1, device_id={"dp": grid.partner(s)}, device_id_type=MESH)

    for step in range(1, n_z):
        pl.semaphore_signal(barrier, inc=1, device_id=at_z(step), device_id_type=MESH)
    for step in range(n_y):
        pl.semaphore_signal(barrier, inc=1, device_id=at_y(1, step), device_id_type=MESH)

    group = (shard * 8) // (2 * n_z * 8 // G)
    cols = pl.ds(pl.multiple_of(group * N, N), N)
    loads = [
        pltpu.make_async_copy(x_any, x_ref, load_sem.at[0]),
        pltpu.make_async_copy(go_any, go_ref, load_sem.at[1]),
        pltpu.make_async_copy(b_any.at[:, :, cols], b_ref, load_sem.at[2]),
        pltpu.make_async_copy(c_any.at[:, :, cols], c_ref, load_sem.at[3]),
    ]
    for copy in loads:
        copy.start()
    for copy in loads:
        copy.wait()
    pl.semaphore_wait(barrier, n_dp - 1 + n_z - 1 + n_y)

    def outgoing(s):
        return remote(
            send_ref.at[s], recv_ref.at[s], es_sem.at[s], er_sem.at[s], {"dp": grid.partner(s)}
        )

    rate = consts_ref[0]
    bias = consts_ref[1]
    gain = gain_ref[...]

    @pl.loop(0, n_block // 2)
    def _(k):
        grads, grad_pre = mixer_pair(
            plan_ref[2 * k], plan_ref[2 * k + 1], pre_ref, starts_ref, rate, bias, gain, x_ref, go_ref, b_ref, c_ref
        )
        for duo in range(4):
            comp_ref[2 * k, :, duo * LANES : (duo + 1) * LANES] = grads[duo][:BLK]
            comp_ref[2 * k + 1, :, duo * LANES : (duo + 1) * LANES] = grads[duo][BLK:]
        gps_ref[2 * k] = grad_pre
        gps_ref[2 * k + 1] = pltpu.roll(grad_pre, LANES - BLK, 1)
        for s in (2 * k, 2 * k + 1):
            send_ref[s] = comp_ref[plan_ref[n_block + s]]
            if n_dp > n_block:
                outgoing(s).start()
            else:
                @pl.when(s < n_dp - 1)
                def _():
                    outgoing(s).start()

    for side in range(2):
        half_ref[side] = gather_lanes([gps_ref[plan_ref[n_block + n_dp + side * n_z + i]] for i in range(n_z)])
    swap = remote(half_ref.at[1 - yh], swap_ref, ws_sem, wr_sem, across)
    swap.start()
    if n_dp > n_block:
        @pl.loop(n_block, n_dp)
        def _(s):
            send_ref[s] = comp_ref[plan_ref[n_block + s]]

            @pl.when(s < n_dp - 1)
            def _():
                outgoing(s).start()

    own = pltpu.make_async_copy(send_ref.at[n_dp - 1], recv_ref.at[n_dp - 1], own_sem)
    own.start()
    swap.wait()
    msg_ref[...] = jnp.concatenate([half_ref[yh], swap_ref[...]], axis=0).astype(BF16)
    copies = []
    for step in range(1, n_z):
        copy = remote(msg_ref, all_ref.at[step], gs_sem.at[step], gr_sem.at[step], at_z(step))
        copy.start()
        copies.append(copy)
    for side in range(2):
        xt_ref[side] = xg_ref[side].astype(F32).T.astype(BF16)
    for step in range(n_z):
        if step:
            copies[step - 1].wait()
        message = (all_ref[step] if step else msg_ref[...]).astype(F32)
        place = (z + n_z - step) % n_z
        heads_ref[yh, place] = message[:8]
        heads_ref[1 - yh, place] = message[8:]
    grad_heads = heads_ref[...].reshape(2 * n_z * 8, heads_ref.shape[-1]).astype(BF16)
    unit = dw_ref.shape[0] // n_dp
    piece = n_y * unit
    for side in range(2):
        product = lax.dot_general(xt_ref[side], grad_heads, NT, preferred_element_type=F32)
        for c in range(2):
            for x in range(n_x):
                low = (c * n_x + x) * piece
                d_ref[c, x, side] = product[low : low + piece]
    copy = remote(d_ref.at[1 - core], e1_ref, cs_sem, cr_sem, sibling)
    copy.start()
    copy.wait()
    a1_ref[...] = d_ref[core] + e1_ref[...]
    copies = []
    for step in range(1, n_x):
        copy = remote(a1_ref.at[(xx + step) % n_x], e2_ref.at[step], xs_sem.at[step], xr_sem.at[step], at_x(step))
        copy.start()
        copies.append(copy)
    total = a1_ref[xx]
    for step, copy in enumerate(copies, 1):
        copy.wait()
        total = total + e2_ref[step]
    a2_ref[...] = total
    copies = []
    for side in range(2):
        for step in range(n_y):
            if side or step:
                rows = pl.ds(pl.multiple_of(((yy + step) % n_y) * unit, unit), unit)
                copy = remote(
                    a2_ref.at[side, rows], e3_ref.at[side, step],
                    ys_sem.at[side, step], yr_sem.at[side, step], at_y(side, step),
                )
                copy.start()
                copies.append((side, step, copy))
    total = a2_ref[0, pl.ds(pl.multiple_of(yy * unit, unit), unit)]
    for side, step, copy in copies:
        copy.wait()
        total = total + e3_ref[side, step]
    low = pl.multiple_of((core * n_x + xx) * piece, piece)
    mine = pl.ds(pl.multiple_of(low + yy * unit, unit), unit)
    dw_ref[mine] = total * scale
    copies = []
    for step in range(1, n_y):
        copy = remote(dw_ref.at[mine], dw_ref.at[mine], fs_sem.at[step], fr_sem.at[step], at_y(0, step))
        copy.start()
        copies.append(copy)
    for copy in copies:
        copy.wait()
    mine = pl.ds(low, piece)
    copies = []
    for step in range(1, n_x):
        copy = remote(dw_ref.at[mine], dw_ref.at[mine], hs_sem.at[step], hr_sem.at[step], at_x(step))
        copy.start()
        copies.append(copy)
    for copy in copies:
        copy.wait()
    side_rows = n_x * piece
    mine = pl.ds(pl.multiple_of(core * side_rows, side_rows), side_rows)
    copy = remote(dw_ref.at[mine], dw_ref.at[mine], ks_sem, kr_sem, sibling)
    copy.start()
    copy.wait()

    @pl.loop(0, n_dp - 1)
    def _(s):
        outgoing(s).wait()

    own.wait()


def mix(grid, scale, plan, pre, starts, consts, gain, x, go, b, c, xg):
    n_block, _, width = x.shape
    n_z, n_x, n_y, n_dp = grid.n_z, grid.n_x, grid.n_y, grid.n_dp
    _, half, feats = xg.shape
    heads = 2 * n_z * 8
    unit = feats // n_dp
    piece = n_y * unit
    dma = pltpu.SemaphoreType.DMA
    vmem = pl.BlockSpec(memory_space=pltpu.VMEM)
    hbm = pl.BlockSpec(memory_space=pl.ANY)
    return pl.pallas_call(
        functools.partial(mixer_kernel, grid, scale, n_block),
        out_shape=(
            jax.ShapeDtypeStruct((n_dp, BLK, width), BF16),
            jax.ShapeDtypeStruct((feats, heads), F32),
        ),
        in_specs=[pl.BlockSpec(memory_space=pltpu.SMEM), vmem, vmem, vmem, vmem, hbm, hbm, hbm, hbm, vmem],
        out_specs=[hbm, vmem],
        scratch_shapes=[
            pltpu.VMEM((n_block, BLK, width), BF16),
            pltpu.VMEM((n_block, BLK, width), BF16),
            pltpu.VMEM((n_block, BLK, N), BF16),
            pltpu.VMEM((n_block, BLK, N), BF16),
            pltpu.VMEM((n_block, BLK, width), BF16),
            pltpu.VMEM((n_dp, BLK, width), BF16),
            pltpu.VMEM((n_block, 8, LANES), F32),
            pltpu.VMEM((2, 8, half), F32),
            pltpu.VMEM((8, half), F32),
            pltpu.VMEM((16, half), BF16),
            pltpu.VMEM((n_z, 16, half), BF16),
            pltpu.VMEM((2, n_z, 8, half), F32),
            pltpu.VMEM((2, feats, half), BF16),
            pltpu.VMEM((2, n_x, 2, piece, heads), F32),
            pltpu.VMEM((n_x, 2, piece, heads), F32),
            pltpu.VMEM((n_x, 2, piece, heads), F32),
            pltpu.VMEM((n_x, 2, piece, heads), F32),
            pltpu.VMEM((2, piece, heads), F32),
            pltpu.VMEM((2, n_y, unit, heads), F32),
            dma((4,)), dma((n_dp,)), dma((n_dp,)), dma, dma, dma((n_z,)), dma((n_z,)), dma, dma,
            dma((n_x,)), dma((n_x,)), dma((2, n_y)), dma((2, n_y)), dma((n_y,)), dma((n_y,)),
            dma((n_x,)), dma((n_x,)), dma, dma, dma,
        ],
        compiler_params=pltpu.CompilerParams(
            collective_id=1, has_side_effects=True, vmem_limit_bytes=48 * 1024 * 1024
        ),
        cost_estimate=pl.CostEstimate(flops=10**9, bytes_accessed=10**7, transcendentals=10**6),
    )(plan, pre, starts, consts, gain, x, go, b, c, xg)


def on_device(
    residual_in, conv_out, b_proj, c_proj, grad_out, doc_starts, dest_plan, dt_weight, dt_bias, decay_rate, skip_gain
):
    n_data = lax.axis_size("dp")
    n_shard = lax.axis_size("shard")
    grid = Grid(n_data, n_shard)
    rows = conv_out.shape[0]
    n_block = rows // BLK
    first_head = lax.axis_index("shard") * 8

    slots = jnp.arange(n_data, dtype=jnp.int32)
    blocks = jnp.arange(n_block, dtype=jnp.int32)
    destinations = jnp.arange(n_data, dtype=jnp.int32)
    by_index = jnp.sum(jnp.where(dest_plan[:, None] == destinations[None, :], blocks[:, None] + 1, 0), axis=0)
    arrived = lax.all_to_all(by_index.reshape(n_data, 1), "dp", split_axis=0, concat_axis=0, tiled=True)[:, 0]

    hits = dest_plan[None, :] == grid.partner(slots)[:, None]
    valid = jnp.any(hits, axis=1)
    earlier = jnp.sum(hits[None, :, :] & (slots[None, :, None] < slots[:, None, None]), axis=(1, 2))
    pick = jnp.clip(earlier + valid.astype(jnp.int32) - 1, 0, n_block - 1)
    block_rank = jnp.sum(jnp.where(hits, earlier[:, None], 0), axis=0)
    order = jnp.sum(jnp.where(block_rank[None, :] == blocks[:, None], blocks[None, :], 0), axis=1)
    plan = jnp.concatenate([order, pick, block_rank]).astype(jnp.int32)

    def here(values):
        return lax.dynamic_slice_in_dim(values, first_head, 8, 0)

    consts = jnp.broadcast_to(jnp.stack([here(decay_rate), here(dt_bias)])[:, :, None], (2, 8, LANES))
    gain = jnp.broadcast_to(jnp.repeat(here(skip_gain), 64)[None, :], (8, 512))
    starts = jnp.pad(doc_starts.reshape(n_block, BLK).astype(F32), ((0, 0), (0, LANES - BLK)))
    starts = jnp.broadcast_to(starts[:, None, :], (n_block, 8, LANES))

    xg, pre = project(grid, residual_in, dt_weight)
    scale = float(rows * n_data) ** (-0.5)
    received, dw = mix(
        grid, scale, plan, pre, starts, consts, gain,
        conv_out.reshape(n_block, BLK, -1), grad_out.reshape(n_block, BLK, -1),
        b_proj.reshape(n_block, BLK, -1), c_proj.reshape(n_block, BLK, -1), xg,
    )
    by_slot = arrived[grid.source(slots)]
    sources = jnp.sum(jnp.where(by_slot[None, :] == blocks[:, None] + 1, slots[None, :], 0), axis=1)
    conv_grad = jnp.take(received, sources, axis=0).reshape(rows, -1)
    return conv_grad, dw


def solution(mesh):
    placed = (
        P(("dp", "shard"), None),
        P("dp", "shard"),
        P("dp", None),
        P("dp", None),
        P("dp", "shard"),
        P("dp"),
        P("dp"),
        P("shard", None),
        P(),
        P(),
        P(),
    )
    return jax.shard_map(
        on_device,
        mesh=mesh,
        in_specs=placed,
        out_specs=(P("dp", "shard"), P("shard", None)),
        check_vma=False,
    )
```

time: 668 us -> 121 us (0.18)
  waiting for transfers between devices: 570 us -> 0.01 us
  Pallas kernels: 0 us -> 92.2 us
  starting transfers between devices: 32.2 us -> 10.4 us
  other arithmetic: 19.6 us -> 5.9 us
  between operations: 14 us -> 0.85 us
  matrix products: 11.8 us -> 0 us
  local copies, waits for them, and re-layouts: 19.7 us -> 11 us
    psum x1 -> x0, waiting for transfers between devices: 259 us -> none  [on_device(): summed = lax.psum(shard_part, 'dp')]
    reduce_scatter x1 -> x0, waiting for transfers between devices: 164 us -> none  [on_device(): lax.psum_scatter(partial_grad, 'shard', scatter_dimension=0, tiled=True)]
    pallas_call x0 -> x2, Pallas kernels: none -> 92.2 us  [the longest x1 62.6 us: mix(): pl.pallas_call(functools.partial(mixer_kernel, grid, scale, n_block), out...]
    all_gather x1 -> x0, waiting for transfers between devices: 90 us -> none  [project(): lax.all_gather(dt_weight, 'shard', axis=0, tiled=True)]
    all_to_all x4 -> x1, waiting for transfers between devices: 56.3 us -> 0.01 us  [on_device(): lax.all_to_all(by_index.reshape(n_data, 1), 'dp', split_axis=0, concat_ax...]
    all_to_all x4 -> x1, starting transfers between devices: 32.1 us -> 10.4 us  [on_device(): lax.all_to_all(by_index.reshape(n_data, 1), 'dp', split_axis=0, concat_ax...]
    dot_general x5 -> x0, matrix products: 11.8 us -> none  [the longest x1 4.48 us: group_grads(): jnp.einsum('cihp,cjhp->chij', ups, vals, preferred_element_type=jnp.float32)]
  transfers between devices with their start and end apart: 7 -> 1, of which waited for: 6 -> 0; matrix products, arithmetic and copies ran while one was open for 4% -> 4% of each run, Pallas kernels for 0% -> 77%
where the time goes in v1:
time: 121 us; the launch traced here: 120 us
  Pallas kernels  92.2 us (76%)
  local copies, waits for them, and re-layouts  11 us (9%)
  starting transfers between devices  10.4 us (9%)
  other arithmetic  5.9 us (5%)
    pallas_call x1, Pallas kernels, mix(): pl.pallas_call(functools.partial(mixer_kernel, grid, scale, n_block), out...  62.6 us
    pallas_call x1, Pallas kernels, project(): pl.pallas_call(functools.partial(project_kernel, grid), out_shape=(jax.Sh...  29.6 us
    all_to_all x1, starting transfers between devices, on_device(): lax.all_to_all(by_index.reshape(n_data, 1), 'dp', split_axis=0, concat_ax...  10.4 us
    unnamed x13, local copies, waits for them, and re-layouts  7.01 us
  transfers between devices with their start and end apart: 1, of which 0 were waited for; matrix products, arithmetic and copies ran while one was open for 4% of the time, Pallas kernels for 77%

profile of v1, /device:TPU:1, one launch (start us, length us, event | category | flops | bytes accessed | tf_op | source)
XLA Modules:
  0.0 120.2 jit_solution(5691913736164196178)
XLA Ops:
  0.6 0.7 select_reduce_fusion.3
  1.4 0.7 copy.15
  2.1 10.4 %all-to-all-start = ((s32[32,1,1]{2,1,0:T(1,128)}), s32[32,1,1]{2,1,0:T(1,128)S(1)}, u32[]{:S(2)}, u32[]{:S(2)}) async-start(s32[32,1,1]{2,1,0:T(1,128)} %copy.15), calls=%async_computation | async-start | bytes 32768 | tf_op jit(solution)/shard_map/all_to_all | solution.py:545
  12.6 0.7 compare_reduce_fusion
  13.3 0.7 convert_reduce_fusion
  14.0 0.8 select_reduce_fusion.1
  14.9 0.1 select_reduce_fusion
  15.0 0.7 dynamic_slice.11
  15.7 0.1 broadcast_in_dim.109
  15.8 0.1 broadcast_in_dim.110
  15.8 0.7 convert_element_type.16
  16.5 0.1 convert_element_type.17
  16.7 0.1 pad_add_fusion.plan_ref
  16.7 0.7 dynamic-slice_bitcast_fusion
  17.5 1.0 copy-done
  18.5 0.8 copy-done.1
  19.3 29.6 %shard_map.122 = (bf16[2,384,256]{2,1,0:T(8,128)(2,1)S(1)}, f32[16,8,128]{2,1,0:T(8,128)S(1)}) custom-call(bf16[48,4096]{1,0:T(8,128)(2,1)S(1)} %copy-done, bf16[256,128]{1,0:T(8,128)(2,1)S(1)} %copy-done.1), custom_call_target="tpu_custom_call" | custom-call | flops 100000000 | bytes 2000000 | tf_op jit(solution)/shard_map/pallas_call | solution.py:189
  48.9 0.1 broadcast_in_dim.108.consts_ref
  49.0 0.0 copy-start.2
  49.0 1.1 copy-done.2
  50.1 1.1 copy-done.3
  51.3 1.1 copy-done.4
  52.4 1.1 copy-done.5
  53.5 62.6 %shard_map.123 = (bf16[32,48,512]{2,1,0:T(8,128)(2,1)S(1)}, f32[256,128]{1,0:T(8,128)S(1)}) custom-call(s32[64]{0:T(128)S(1)} %pad_add_fusion.plan_ref, f32[16,8,128]{2,1,0:T(8,128)S(1)} %get-tuple-element.6.pre_ref, f32[16,8,128]{2,1,0:T(8,128)S(1)} %broadcast_in_dim.107.starts_ref, f32[2,8,128]{2,1,0:T(8,128)S(1)} %broadcast_in_dim.108.consts_ref, ...), custom_call_target="tpu_custom_call" | custom-call | flops 1000000000 | bytes 10000000 | tf_op jit(solution)/shard_map/pallas_call | solution.py:492
  116.2 0.7 reduce
  116.8 0.7 gather_fusion
  117.5 0.2 select_reduce_fusion.2
  117.8 0.1 broadcast_in_dim.100
  117.8 0.1 broadcast_in_dim.101
  117.9 0.6 gather_fusion.1
  118.5 1.1 bitcast_select_fusion
  119.6 0.7 copy.17
  (19 shorter events, 0.1 us)
Async XLA Ops:
  2.1 114.1 %all-to-all-start = ((s32[32,1,1]{2,1,0:T(1,128)}), s32[32,1,1]{2,1,0:T(1,128)S(1)}, u32[]{:S(2)}, u32[]{:S(2)}) async-start(s32[32,1,1]{2,1,0:T(1,128)} %copy.15), calls=%async_computation | async-start | bytes 32768 | tf_op jit(solution)/shard_map/all_to_all | solution.py:545
  17.5 1.0 copy-start
  18.5 0.8 copy-start.1
  49.0 1.1 copy-start.2
  50.1 1.1 copy-start.3
  51.3 1.1 copy-start.4
  52.4 1.1 copy-start.5

commit v2 on v1

v2 whole, which is shorter than its diff:
```python
import functools

import jax
import jax.numpy as jnp
from jax import lax
from jax.experimental import pallas as pl
from jax.experimental.pallas import tpu as pltpu
from jax.sharding import PartitionSpec as P

N = 128
G = 4
BLK = 48
LANES = 128
MESH = pl.DeviceIdType.MESH
F32 = jnp.float32
BF16 = jnp.bfloat16
NT = (((1,), (1,)), ((), ()))
NN = (((1,), (0,)), ((), ()))
N_YHI = 2
PAIR = 2 * BLK
TILES = 13
FAR = -1e30


class Grid:
    def __init__(self, n_dp, n_shard):
        self.n_dp = n_dp
        self.n_z = n_shard // N_YHI
        self.n_core = 2
        rest = n_dp // 2
        self.n_hb = 2 if rest >= 2 else 1
        rest //= self.n_hb
        self.n_x = min(rest, 4)
        self.n_lb = rest // self.n_x
        self.n_y = self.n_hb * self.n_lb

    def here(self):
        dp = lax.axis_index("dp")
        shard = lax.axis_index("shard")
        core = lax.rem(dp, self.n_core)
        x = lax.rem(dp // self.n_core, self.n_x)
        y = dp // (self.n_core * self.n_x)
        return dp, y, x, core, shard // self.n_z, lax.rem(shard, self.n_z)

    def dp_of(self, y, x, core):
        return (y * self.n_x + x) * self.n_core + core

    def partner(self, s):
        _, y, x, core, _, _ = self.here()
        mc = self.n_core - 1 - s % self.n_core
        mx = self.n_x - 1 - (s // self.n_core) % self.n_x
        t = s // (self.n_core * self.n_x)
        hb = y // self.n_lb
        lb = y % self.n_lb
        hb2 = (hb + self.n_hb - 1 + t // self.n_lb) % self.n_hb
        lb2 = (lb + self.n_lb - 1 + t % self.n_lb) % self.n_lb
        if self.n_lb == 1:
            lb2 = lb
        return self.dp_of(hb2 * self.n_lb + lb2, (x + mx) % self.n_x, (core + mc) % self.n_core)


def remote(src, dst, send, recv, device):
    return pltpu.make_async_remote_copy(
        src_ref=src, dst_ref=dst, send_sem=send, recv_sem=recv, device_id=device, device_id_type=MESH
    )


def lanes():
    return lax.broadcasted_iota(jnp.int32, (8, LANES), 1)


def spread_lanes(whole, low):
    width = whole.shape[1]
    if width % LANES:
        return jnp.pad(whole[:, low : low + PAIR], ((0, 0), (0, LANES - PAIR)))
    tile, off = low // LANES, low % LANES
    first = whole[:, tile * LANES : (tile + 1) * LANES]
    if off == 0:
        return first
    first = pltpu.roll(first, LANES - off, 1)
    if off + PAIR <= LANES:
        return first
    second = pltpu.roll(whole[:, (tile + 1) * LANES : (tile + 2) * LANES], LANES - off, 1)
    return jnp.where(lanes() < LANES - off, first, second)


def gather_lanes(pieces):
    width = len(pieces) * PAIR
    if width % LANES:
        return jnp.concatenate([p[:, :PAIR] for p in pieces], axis=1)
    lane = lanes()
    tiles = [jnp.zeros((8, LANES), F32) for _ in range(width // LANES)]
    for index, piece in enumerate(pieces):
        low = index * PAIR
        tile, off = low // LANES, low % LANES
        moved = pltpu.roll(piece, off, 1) if off else piece
        tiles[tile] = jnp.where((lane >= off) & (lane < off + PAIR), moved, tiles[tile])
        if off + PAIR > LANES:
            tiles[tile + 1] = jnp.where(lane < off + PAIR - LANES, moved, tiles[tile + 1])
    return jnp.concatenate(tiles, axis=1)


def triangle(kind):
    row = lax.broadcasted_iota(jnp.int32, (LANES, LANES), 0)
    col = lax.broadcasted_iota(jnp.int32, (LANES, LANES), 1)
    same = (row < BLK) == (col < BLK)
    if kind == "all":
        keep = row <= col
    elif kind == "ahead":
        keep = (row <= col) & same
    else:
        keep = (row >= col) & same
    return jnp.where(keep, 1.0, 0.0).astype(F32)


def causal(transposed):
    row = lax.broadcasted_iota(jnp.int32, (PAIR, LANES), 0)
    col = lax.broadcasted_iota(jnp.int32, (PAIR, LANES), 1)
    same = ((row < BLK) == (col < BLK)) & (col < PAIR)
    return jnp.where(same & ((row <= col) if transposed else (col <= row)), 0.0, FAR).astype(F32)


def exact_dot(a, b):
    return lax.dot_general(a, b, NN, preferred_element_type=F32, precision=lax.Precision.HIGHEST)


def split_dot(a, b):
    high = b.astype(BF16)
    low = (b - high.astype(F32)).astype(BF16)
    return lax.dot_general(a, high, NT, preferred_element_type=F32) + lax.dot_general(
        a, low, NT, preferred_element_type=F32
    )


def columns_of(*rows):
    filled = LANES - 8 * len(rows)
    return jnp.concatenate(list(rows) + [jnp.zeros((filled, LANES), F32)], axis=0).T


def score_pair(starts, b, c):
    pad = jnp.zeros((LANES - PAIR, N), BF16)
    segment = lax.dot_general(
        starts.astype(BF16), triangle("all").astype(BF16), NN, preferred_element_type=F32
    )
    segment = jnp.where(lanes() < PAIR, segment, -1.0)
    same = columns_of(segment)[:PAIR, 0:1] == segment[0:1]
    score = lax.dot_general(c, jnp.concatenate([b, pad], axis=0), NT, preferred_element_type=F32)
    score_t = lax.dot_general(b, jnp.concatenate([c, pad], axis=0), NT, preferred_element_type=F32)
    return (
        jnp.where(same & (causal(False) == 0.0), score, 0.0),
        jnp.where(same & (causal(True) == 0.0), score_t, 0.0),
    )


def pack_scores(score_t):
    lane = lax.broadcasted_iota(jnp.int32, (16, LANES), 1)

    def packed(first, second, third):
        return jnp.where(lane < 48, first, jnp.where(lane < 96, second, third))

    return (
        packed(score_t[0:16], pltpu.roll(score_t[16:32], 48, 1), pltpu.roll(score_t[32:48], 64, 1)),
        packed(pltpu.roll(score_t[48:64], 80, 1), score_t[64:80], pltpu.roll(score_t[80:96], 16, 1)),
    )


def unpack_scores(one, two):
    return jnp.concatenate(
        [one, pltpu.roll(one, 80, 1), pltpu.roll(one, 64, 1), pltpu.roll(two, 48, 1), two, pltpu.roll(two, 112, 1)],
        axis=0,
    )


def mixer_pair(pre, score, score_t, rate, bias, x_of, go_of):
    lane = lanes()
    gate = jnp.where(lane < PAIR, pre + bias, 0.0)
    e = jnp.exp(-jnp.abs(gate))
    series = e * (1.0 - e * (0.5 - e * (1.0 / 3.0 - e * (0.25 - e * 0.2))))
    log1p = jnp.where(e < 0.02, series, jnp.log(1.0 + e))
    step = jnp.maximum(gate, 0.0) + log1p
    sig = jnp.where(gate >= 0, 1.0, e) / (1.0 + e)
    ratio = jnp.where((gate < 0) & (e < 1e-6), 1.0, sig / jnp.maximum(step, 1e-20))
    level = exact_dot(jnp.where(lane < PAIR, -step * rate, 0.0), triangle("ahead"))
    cols = columns_of(level, step)
    away, away_t = causal(False), causal(True)
    pad = jnp.zeros((LANES - PAIR, LANES), BF16)
    low_half = lax.broadcasted_iota(jnp.int32, (PAIR, LANES), 1) < 64
    by_value, by_grad = [], []
    for duo in range(4):
        mix, mix_t = [], []
        for head in (2 * duo, 2 * duo + 1):
            level_col = cols[:PAIR, head : head + 1]
            step_col = cols[:PAIR, 8 + head : 9 + head]
            level_row = level[head : head + 1]
            step_row = step[head : head + 1]
            mix.append((score * jnp.exp(level_col - level_row + away) * step_row).astype(BF16))
            mix_t.append((score_t * jnp.exp(level_row - level_col + away_t) * step_col).astype(BF16))
        x = x_of(duo)
        go = go_of(duo)
        y = lax.dot_general(
            jnp.concatenate(mix, axis=0), jnp.concatenate([x, pad], axis=0), NN, preferred_element_type=F32
        )
        gv = lax.dot_general(
            jnp.concatenate(mix_t, axis=0), jnp.concatenate([go, pad], axis=0), NN, preferred_element_type=F32
        )
        by_value.append(x.astype(F32) * jnp.where(low_half, gv[:PAIR], gv[PAIR:]))
        by_grad.append(go.astype(F32) * jnp.where(low_half, y[:PAIR], y[PAIR:]))
    zeros = jnp.zeros((LANES - PAIR, 4 * LANES), F32)
    head_of = lax.broadcasted_iota(jnp.int32, (8, 4 * LANES), 1) // 64
    pick = jnp.where(head_of == lax.broadcasted_iota(jnp.int32, (8, 4 * LANES), 0), 1.0, 0.0).astype(BF16)
    inflow = split_dot(pick, jnp.concatenate([jnp.concatenate(by_value, axis=1), zeros], axis=0))
    outflow = split_dot(pick, jnp.concatenate([jnp.concatenate(by_grad, axis=1), zeros], axis=0))
    grad_log = exact_dot(outflow - inflow, triangle("behind"))
    return inflow * ratio - rate * grad_log * sig, level, step


def per_head(ref, first_head):
    row = lax.broadcasted_iota(jnp.int32, (8, LANES), 0)
    out = jnp.zeros((8, LANES), F32)
    for head in range(8):
        out = jnp.where(row == head, ref[first_head + head], out)
    return out


def main_kernel(
    grid, n_block,
    tokens_any, w_ref, x_any, go_any, b_any, c_any, starts_ref, plan_ref, bias_ref, rate_ref,
    got_ref, notes_ref, dw_ref,
    xg_ref, wo_ref, full_ref, part_ref, rs_ref, give_ref, take_ref,
    x_ref, go_ref, b_ref, c_ref, send_ref, pre_ref, segs_ref, score_ref, score_t_ref, tile_ref, level_ref, note_ref,
    gps_ref, half_ref, swap_ref, msg_ref, all_ref, heads_ref, xt_ref, d_ref, e1_ref, a1_ref, e2_ref, a2_ref, e3_ref,
    local_sem, load_sem, vs_sem, vr_sem, ts_sem, tr_sem, ps_sem, pr_sem, ss_sem, sr_sem,
    es_sem, er_sem, ns_sem, nr_sem, ws_sem, wr_sem, gs_sem, gr_sem, cs_sem, cr_sem, xs_sem, xr_sem, ys_sem, yr_sem,
    fs_sem, fr_sem, hs_sem, hr_sem, ks_sem, kr_sem, own_sem,
):
    n_z, n_x, n_y, n_dp = grid.n_z, grid.n_x, grid.n_y, grid.n_dp
    dp, yy, xx, core, yh, z = grid.here()
    shard = yh * n_z + z
    other = (1 - yh) * n_z + z
    across = {"shard": other}
    sibling = {"dp": grid.dp_of(yy, xx, 1 - core)}
    feats = w_ref.shape[0]
    per_half = n_z // 2

    def at_z(step):
        return {"shard": yh * n_z + (z + step) % n_z}

    def at_x(step):
        return {"dp": grid.dp_of(yy, (xx + step) % n_x, core)}

    def at_y(side, step):
        place = grid.dp_of((yy + step) % n_y, xx, core)
        return {"dp": place, "shard": shard if side == 0 else other}

    barrier = pltpu.get_barrier_semaphore()
    for step in range(1, n_z):
        pl.semaphore_signal(barrier, inc=1, device_id=at_z(step), device_id_type=MESH)
    for step in range(n_y):
        pl.semaphore_signal(barrier, inc=1, device_id=at_y(1, step), device_id_type=MESH)

    @pl.loop(0, n_dp - 1)
    def _(s):
        pl.semaphore_signal(barrier, inc=1, device_id={"dp": grid.partner(s)}, device_id_type=MESH)

    def feature_columns(side, step):
        owner = (yh if side == 0 else 1 - yh) * n_z + (z + step) % n_z
        return tokens_any.at[:, pl.ds(pl.multiple_of(owner * feats, feats), feats)]

    mine = pl.ds(pl.multiple_of(z * BLK, BLK), BLK)
    group = (shard * 8) // (2 * n_z * 8 // G)
    cols = pl.ds(pl.multiple_of(group * N, N), N)
    loads = [
        pltpu.make_async_copy(b_any.at[:, :, cols], b_ref, load_sem.at[2]),
        pltpu.make_async_copy(c_any.at[:, :, cols], c_ref, load_sem.at[3]),
        pltpu.make_async_copy(go_any, go_ref, load_sem.at[1]),
        pltpu.make_async_copy(x_any, x_ref, load_sem.at[0]),
    ]
    for side in range(2):
        loads.append(pltpu.make_async_copy(feature_columns(side, 0), xg_ref.at[side, mine], local_sem.at[side]))
    for copy in loads:
        copy.start()
    pl.semaphore_wait(barrier, n_dp - 1 + n_z - 1 + n_y)

    weight_swap = remote(w_ref, wo_ref, vs_sem, vr_sem, across)
    weight_swap.start()
    token_copies = []
    for step in range(1, n_z):
        for side in range(2):
            copy = remote(
                feature_columns(side, step), xg_ref.at[side, mine],
                ts_sem.at[step, side], tr_sem.at[step, side], at_z(step),
            )
            copy.start()
            token_copies.append(copy)

    for copy in loads[:3]:
        copy.wait()
    marks = jnp.broadcast_to(starts_ref[...].astype(F32), (8, n_block * BLK))
    for q in range(n_block // 2):
        segs_ref[q] = spread_lanes(marks, q * PAIR)

    def both(ref, q, low):
        return jnp.concatenate([ref[2 * q, :, pl.ds(low, LANES)], ref[2 * q + 1, :, pl.ds(low, LANES)]], axis=0)

    @pl.loop(0, n_block // 2)
    def _(q):
        score, score_t = score_pair(segs_ref[q], both(b_ref, q, 0), both(c_ref, q, 0))
        score_ref[q] = score
        score_t_ref[q] = score_t
        one, two = pack_scores(score_t)
        tile_ref[2 * q] = one.astype(BF16)
        tile_ref[2 * q + 1] = two.astype(BF16)

    def label_of(s):
        target = grid.partner(s)
        label = jnp.int32(0)
        for block in range(n_block):
            label = label + jnp.where(plan_ref[block] == target, block + 1, 0)
        return label

    def outgoing(s):
        return remote(send_ref.at[s], got_ref.at[s], es_sem.at[s], er_sem.at[s], {"dp": grid.partner(s)})

    def noted(s):
        return remote(note_ref.at[s], notes_ref.at[s], ns_sem.at[s], nr_sem.at[s], {"dp": grid.partner(s)})

    @pl.loop(0, n_dp)
    def _(s):
        block = jnp.clip(label_of(s) - 1, 0, n_block - 1)
        whole = go_ref[block]
        for r in range(3):
            for t in range(4):
                send_ref[s, 4 * r + t] = whole[16 * r : 16 * r + 16, t * LANES : (t + 1) * LANES]
        send_ref[s, TILES - 1] = tile_ref[block]

        @pl.when(s < n_dp - 1)
        def _():
            outgoing(s).start()

    own = pltpu.make_async_copy(send_ref.at[n_dp - 1], got_ref.at[n_dp - 1], own_sem.at[0])
    own.start()

    w_here = w_ref[...].astype(F32).T.astype(BF16)
    for copy in loads[3:]:
        copy.wait()
    weight_swap.wait()
    w_other = wo_ref[...].astype(F32).T.astype(BF16)
    for copy in token_copies:
        copy.wait()
    full_ref[...] = lax.dot_general(w_here, xg_ref[0], NT, preferred_element_type=F32) + lax.dot_general(
        w_other, xg_ref[1], NT, preferred_element_type=F32
    )
    copies = []
    for step in list(range(1, n_z)) + [0]:
        for side in range(2):
            owner = (yh if side == 0 else 1 - yh) * n_z + (z + step) % n_z
            part_ref[step, side * 8 : (side + 1) * 8] = full_ref[pl.ds(pl.multiple_of(owner * 8, 8), 8)]
        if step:
            copy = remote(part_ref.at[step], rs_ref.at[step], ps_sem.at[step], pr_sem.at[step], at_z(step))
            copy.start()
            copies.append(copy)
    for side in range(2):
        xt_ref[side] = xg_ref[side].astype(F32).T.astype(BF16)
    total = part_ref[0]
    for step, copy in enumerate(copies, 1):
        copy.wait()
        total = total + rs_ref[step]
    give_ref[...] = total[8:]
    logit_swap = remote(give_ref, take_ref, ss_sem, sr_sem, across)
    logit_swap.start()
    for q in range(per_half):
        pre_ref[yh * per_half + q] = spread_lanes(total[:8], q * PAIR)

    rate = per_head(rate_ref, shard * 8)
    bias = per_head(bias_ref, shard * 8)
    lane = lanes()

    def work(q):
        grad_pre, level, step = mixer_pair(
            pre_ref[q], score_ref[q], score_t_ref[q], rate, bias,
            lambda duo: both(x_ref, q, duo * LANES), lambda duo: both(go_ref, q, duo * LANES),
        )
        gps_ref[q] = grad_pre
        level_ref[2 * q] = jnp.where(lane < BLK, level, pltpu.roll(step, BLK, 1))
        level_ref[2 * q + 1] = jnp.where(lane < BLK, pltpu.roll(level, LANES - BLK, 1), step)

    @pl.loop(0, per_half // 2)
    def _(q):
        work(yh * per_half + q)

    logit_swap.wait()
    others = take_ref[...]
    for q in range(per_half):
        pre_ref[(1 - yh) * per_half + q] = spread_lanes(others, q * PAIR)

    @pl.loop(0, per_half)
    def _(q):
        work((1 - yh) * per_half + q)

    half_ref[0] = gather_lanes([gps_ref[(1 - yh) * per_half + i] for i in range(per_half)])
    grad_swap = remote(half_ref.at[0], swap_ref, ws_sem, wr_sem, across)
    grad_swap.start()

    @pl.loop(per_half // 2, per_half)
    def _(q):
        work(yh * per_half + q)

    mine_half = gather_lanes([gps_ref[yh * per_half + i] for i in range(per_half)])
    grad_swap.wait()
    msg_ref[...] = jnp.concatenate([mine_half, swap_ref[...]], axis=0).astype(BF16)
    copies = []
    for step in range(1, n_z):
        copy = remote(msg_ref, all_ref.at[step], gs_sem.at[step], gr_sem.at[step], at_z(step))
        copy.start()
        copies.append(copy)

    @pl.loop(0, n_dp)
    def _(s):
        label = label_of(s)
        note_ref[s] = jnp.where(lane < PAIR, level_ref[jnp.clip(label - 1, 0, n_block - 1)], label.astype(F32))

        @pl.when(s < n_dp - 1)
        def _():
            noted(s).start()

    own_note = pltpu.make_async_copy(note_ref.at[n_dp - 1], notes_ref.at[n_dp - 1], own_sem.at[1])
    own_note.start()

    for step in range(n_z):
        if step:
            copies[step - 1].wait()
        message = (all_ref[step] if step else msg_ref[...]).astype(F32)
        place = (z + n_z - step) % n_z
        heads_ref[yh, place] = message[:8]
        heads_ref[1 - yh, place] = message[8:]
    grad_heads = heads_ref[...].reshape(2 * n_z * 8, heads_ref.shape[-1]).astype(BF16)
    unit = dw_ref.shape[0] // n_dp
    piece = n_y * unit
    for side in range(2):
        product = lax.dot_general(xt_ref[side], grad_heads, NT, preferred_element_type=F32)
        for c in range(2):
            for x in range(n_x):
                low = (c * n_x + x) * piece
                d_ref[c, x, side] = product[low : low + piece]
    copy = remote(d_ref.at[1 - core], e1_ref, cs_sem, cr_sem, sibling)
    copy.start()
    copy.wait()
    a1_ref[...] = d_ref[core] + e1_ref[...]
    copies = []
    for step in range(1, n_x):
        copy = remote(a1_ref.at[(xx + step) % n_x], e2_ref.at[step], xs_sem.at[step], xr_sem.at[step], at_x(step))
        copy.start()
        copies.append(copy)
    total = a1_ref[xx]
    for step, copy in enumerate(copies, 1):
        copy.wait()
        total = total + e2_ref[step]
    a2_ref[...] = total
    copies = []
    for side in range(2):
        for step in range(n_y):
            if side or step:
                rows = pl.ds(pl.multiple_of(((yy + step) % n_y) * unit, unit), unit)
                copy = remote(
                    a2_ref.at[side, rows], e3_ref.at[side, step],
                    ys_sem.at[side, step], yr_sem.at[side, step], at_y(side, step),
                )
                copy.start()
                copies.append((side, step, copy))
    total = a2_ref[0, pl.ds(pl.multiple_of(yy * unit, unit), unit)]
    for side, step, copy in copies:
        copy.wait()
        total = total + e3_ref[side, step]
    low = pl.multiple_of((core * n_x + xx) * piece, piece)
    mine = pl.ds(pl.multiple_of(low + yy * unit, unit), unit)
    dw_ref[mine] = total * (float(n_dp * n_block * BLK) ** -0.5)
    copies = []
    for step in range(1, n_y):
        copy = remote(dw_ref.at[mine], dw_ref.at[mine], fs_sem.at[step], fr_sem.at[step], at_y(0, step))
        copy.start()
        copies.append(copy)
    for copy in copies:
        copy.wait()
    mine = pl.ds(low, piece)
    copies = []
    for step in range(1, n_x):
        copy = remote(dw_ref.at[mine], dw_ref.at[mine], hs_sem.at[step], hr_sem.at[step], at_x(step))
        copy.start()
        copies.append(copy)
    for copy in copies:
        copy.wait()
    side_rows = n_x * piece
    mine = pl.ds(pl.multiple_of(core * side_rows, side_rows), side_rows)
    copy = remote(dw_ref.at[mine], dw_ref.at[mine], ks_sem, kr_sem, sibling)
    copy.start()
    copy.wait()

    @pl.loop(0, n_dp - 1)
    def _(s):
        noted(s).wait()
        outgoing(s).wait()

    own.wait()
    own_note.wait()


def main_call(grid, tokens, weight, x, go, b, c, starts, plan, bias, rate):
    n_block, _, width = x.shape
    n_z, n_x, n_y, n_dp = grid.n_z, grid.n_x, grid.n_y, grid.n_dp
    half = n_z * BLK
    feats, heads = weight.shape
    unit = feats // n_dp
    piece = n_y * unit
    n_pair = n_block // 2
    dma = pltpu.SemaphoreType.DMA
    vmem = pl.BlockSpec(memory_space=pltpu.VMEM)
    smem = pl.BlockSpec(memory_space=pltpu.SMEM)
    hbm = pl.BlockSpec(memory_space=pl.ANY)
    return pl.pallas_call(
        functools.partial(main_kernel, grid, n_block),
        out_shape=(
            jax.ShapeDtypeStruct((n_dp, TILES, 16, LANES), BF16),
            jax.ShapeDtypeStruct((n_dp, 8, LANES), F32),
            jax.ShapeDtypeStruct((feats, heads), F32),
        ),
        in_specs=[hbm, vmem, hbm, hbm, hbm, hbm, vmem, smem, smem, smem],
        out_specs=[hbm, hbm, vmem],
        scratch_shapes=[
            pltpu.VMEM((2, half, feats), BF16),
            pltpu.VMEM((feats, heads), BF16),
            pltpu.VMEM((heads, half), F32),
            pltpu.VMEM((n_z, 16, half), F32),
            pltpu.VMEM((n_z, 16, half), F32),
            pltpu.VMEM((8, half), F32),
            pltpu.VMEM((8, half), F32),
            pltpu.VMEM((n_block, BLK, width), BF16),
            pltpu.VMEM((n_block, BLK, width), BF16),
            pltpu.VMEM((n_block, BLK, N), BF16),
            pltpu.VMEM((n_block, BLK, N), BF16),
            pltpu.VMEM((n_dp, TILES, 16, LANES), BF16),
            pltpu.VMEM((n_pair, 8, LANES), F32),
            pltpu.VMEM((n_pair, 8, LANES), F32),
            pltpu.VMEM((n_pair, PAIR, LANES), F32),
            pltpu.VMEM((n_pair, PAIR, LANES), F32),
            pltpu.VMEM((n_block, 16, LANES), BF16),
            pltpu.VMEM((n_block, 8, LANES), F32),
            pltpu.VMEM((n_dp, 8, LANES), F32),
            pltpu.VMEM((n_pair, 8, LANES), F32),
            pltpu.VMEM((1, 8, half), F32),
            pltpu.VMEM((8, half), F32),
            pltpu.VMEM((16, half), BF16),
            pltpu.VMEM((n_z, 16, half), BF16),
            pltpu.VMEM((2, n_z, 8, half), F32),
            pltpu.VMEM((2, feats, half), BF16),
            pltpu.VMEM((2, n_x, 2, piece, heads), F32),
            pltpu.VMEM((n_x, 2, piece, heads), F32),
            pltpu.VMEM((n_x, 2, piece, heads), F32),
            pltpu.VMEM((n_x, 2, piece, heads), F32),
            pltpu.VMEM((2, piece, heads), F32),
            pltpu.VMEM((2, n_y, unit, heads), F32),
            dma((2,)), dma((4,)), dma, dma, dma((n_z, 2)), dma((n_z, 2)), dma((n_z,)), dma((n_z,)), dma, dma,
            dma((n_dp,)), dma((n_dp,)), dma((n_dp,)), dma((n_dp,)), dma, dma, dma((n_z,)), dma((n_z,)), dma, dma,
            dma((n_x,)), dma((n_x,)), dma((2, n_y)), dma((2, n_y)), dma((n_y,)), dma((n_y,)),
            dma((n_x,)), dma((n_x,)), dma, dma, dma((2,)),
        ],
        compiler_params=pltpu.CompilerParams(
            collective_id=0, has_side_effects=True, vmem_limit_bytes=60 * 1024 * 1024
        ),
        cost_estimate=pl.CostEstimate(flops=10**9, bytes_accessed=10**7, transcendentals=10**6),
    )(tokens, weight, x, go, b, c, starts, plan, bias, rate)


def finish_kernel(source_ref, gain_ref, got_ref, note_ref, dw_in_ref, out_ref, dw_ref):
    shard = lax.axis_index("shard")
    lane = lanes()
    dw_ref[...] = dw_in_ref[...]
    away_t = causal(True)
    pad = jnp.zeros((LANES - PAIR, LANES), BF16)
    low_half = lax.broadcasted_iota(jnp.int32, (PAIR, LANES), 1) < 64

    @pl.loop(0, out_ref.shape[0] // 2)
    def _(q):
        last = got_ref.shape[0] - 1
        first = jnp.clip(source_ref[2 * q], 0, last)
        second = jnp.clip(source_ref[2 * q + 1], 0, last)
        one, two = note_ref[first], note_ref[second]
        level = jnp.where(lane < BLK, one, jnp.where(lane < PAIR, pltpu.roll(two, BLK, 1), 0.0))
        step = jnp.where(lane < BLK, pltpu.roll(one, LANES - BLK, 1), jnp.where(lane < PAIR, two, 0.0))
        cols = columns_of(level, step)
        score_t = unpack_scores(
            got_ref[first, TILES - 1].astype(F32), got_ref[second, TILES - 1].astype(F32)
        )
        for duo in range(4):
            mix_t = []
            for head in (2 * duo, 2 * duo + 1):
                level_col = cols[:PAIR, head : head + 1]
                step_col = cols[:PAIR, 8 + head : 9 + head]
                mix_t.append(
                    (score_t * jnp.exp(level[head : head + 1] - level_col + away_t) * step_col).astype(BF16)
                )
            go = jnp.concatenate(
                [got_ref[first, 4 * r + duo] for r in range(3)] + [got_ref[second, 4 * r + duo] for r in range(3)],
                axis=0,
            )
            gv = lax.dot_general(
                jnp.concatenate(mix_t, axis=0), jnp.concatenate([go, pad], axis=0), NN, preferred_element_type=F32
            )
            gv = jnp.where(low_half, gv[:PAIR], gv[PAIR:])
            gain = jnp.where(low_half, gain_ref[shard * 8 + 2 * duo], gain_ref[shard * 8 + 2 * duo + 1])
            grad = (gv + gain * go.astype(F32)).astype(BF16)
            out_ref[2 * q, :, duo * LANES : (duo + 1) * LANES] = grad[:BLK]
            out_ref[2 * q + 1, :, duo * LANES : (duo + 1) * LANES] = grad[BLK:]


def finish(sources, gain, got, notes, dw, n_block):
    vmem = pl.BlockSpec(memory_space=pltpu.VMEM)
    smem = pl.BlockSpec(memory_space=pltpu.SMEM)
    return pl.pallas_call(
        finish_kernel,
        out_shape=(
            jax.ShapeDtypeStruct((n_block, BLK, 4 * LANES), BF16),
            jax.ShapeDtypeStruct(dw.shape, F32),
        ),
        in_specs=[smem, smem, vmem, vmem, vmem],
        out_specs=[vmem, vmem],
        compiler_params=pltpu.CompilerParams(vmem_limit_bytes=60 * 1024 * 1024),
        cost_estimate=pl.CostEstimate(flops=10**8, bytes_accessed=4 * 10**6, transcendentals=10**6),
    )(sources, gain, got, notes, dw)


def on_device(
    residual_in, conv_out, b_proj, c_proj, grad_out, doc_starts, dest_plan, dt_weight, dt_bias, decay_rate, skip_gain
):
    n_data = lax.axis_size("dp")
    grid = Grid(n_data, lax.axis_size("shard"))
    rows = conv_out.shape[0]
    n_block = rows // BLK

    def blocked(values):
        return values.reshape(n_block, BLK, -1)

    got, notes, dw = main_call(
        grid, residual_in, dt_weight, blocked(conv_out), blocked(grad_out), blocked(b_proj), blocked(c_proj),
        doc_starts.reshape(1, rows), dest_plan, dt_bias, decay_rate,
    )
    labels = notes[:, 0, LANES - 1].astype(jnp.int32)
    slots = jnp.arange(n_data, dtype=jnp.int32)
    wanted = jnp.arange(1, n_block + 1, dtype=jnp.int32)
    sources = jnp.sum(jnp.where(labels[None, :] == wanted[:, None], slots[None, :], 0), axis=1)
    conv_grad, dw = finish(sources, skip_gain, got, notes, dw, n_block)
    return conv_grad.reshape(rows, -1), dw


def solution(mesh):
    placed = (
        P(("dp", "shard"), None),
        P("dp", "shard"),
        P("dp", None),
        P("dp", None),
        P("dp", "shard"),
        P("dp"),
        P("dp"),
        P("shard", None),
        P(),
        P(),
        P(),
    )
    return jax.shard_map(
        on_device,
        mesh=mesh,
        in_specs=placed,
        out_specs=(P("dp", "shard"), P("shard", None)),
        check_vma=False,
    )
```

time: 121 us -> 104 us (0.86)
  starting transfers between devices: 10.4 us -> 0 us
  local copies, waits for them, and re-layouts: 11 us -> 1.27 us
  Pallas kernels: 92.2 us -> 99.7 us
  other arithmetic: 5.9 us -> 2.37 us
    all_to_all x1 -> x0, starting transfers between devices: 10.4 us -> none  [on_device(): lax.all_to_all(by_index.reshape(n_data, 1), 'dp', split_axis=0, concat_ax...]
    pallas_call x2, Pallas kernels: 92.2 us -> 99.7 us  [the longest x1 92.4 us: main_call(): pl.pallas_call(functools.partial(main_kernel, grid, n_block), out_shape=(...]
    unnamed x13 -> x0, local copies, waits for them, and re-layouts: 7.01 us -> none
    reduce_sum x5 -> x1, other arithmetic: 2.56 us -> 0.73 us  [on_device(): jnp.sum(jnp.where(labels[None, :] == wanted[:, None], slots[None, :], 0),...]
    gather x2 -> x0, local copies, waits for them, and re-layouts: 1.31 us -> none  [the longest x1 0.71 us: on_device(): by_slot = arrived[grid.source(slots)]]
    reshape x0 -> x1, local copies, waits for them, and re-layouts: none -> 1.27 us  [on_device(): doc_starts.reshape(1, rows)]
  transfers between devices with their start and end apart: 1 -> 0, of which waited for: 0 -> 0; matrix products, arithmetic and copies ran while one was open for 4% -> 0% of each run, Pallas kernels for 77% -> 0%
where the time goes in v2:
time: 104 us
  Pallas kernels  99.7 us (96%)
  other arithmetic  2.37 us (2%)
  local copies, waits for them, and re-layouts  1.27 us (1%)
    pallas_call x1, Pallas kernels, main_call(): pl.pallas_call(functools.partial(main_kernel, grid, n_block), out_shape=(...  92.4 us
    pallas_call x1, Pallas kernels, finish(): pl.pallas_call(finish_kernel, out_shape=(jax.ShapeDtypeStruct((n_block, B...  7.3 us

profile of v2, /device:TPU:1, one launch (start us, length us, event | category | flops | bytes accessed | tf_op | source)
XLA Modules:
  0.0 104.0 jit_solution(3470615946280204655)
XLA Ops:
  0.6 1.3 %reshape.36.starts_ref = s32[1,768]{1,0:T(1,128)} reshape(s32[768]{0:T(1024)} %param.16) | data formatting | bytes 6144 | tf_op jit(solution)/shard_map/reshape | solution.py:644
  1.9 92.4 %shard_map.122 = (bf16[32,13,16,128]{3,2,1,0:T(8,128)(2,1)}, f32[32,8,128]{2,1,0:T(8,128)}, f32[256,128]{1,0:T(8,128)}) custom-call(bf16[48,4096]{1,0:T(8,128)(2,1)} %tokens_any.1, bf16[256,128]{1,0:T(8,128)(2,1)} %w_ref.1, bf16[16,48,512]{2,1,0:T(8,128)(2,1)} %bitcast.5, bf16[16,48,512]{2,1,0:T(8,128)(2,1)} %bitcast.6, bf16[16,48,512]{2,1,0:T(8,128)(2,1)} %bitcast.7, ...), custom_call_target="tpu_custom_call" | custom-call | flops 1000000000 | bytes 10000000 | tf_op jit(solution)/shard_map/pallas_call | solution.py:519
  94.4 1.6 %convert_reduce_fusion = s32[32]{0:T(128)S(1)} fusion(f32[32,8,128]{2,1,0:T(8,128)} %get-tuple-element.7.note_ref), kind=kLoop, calls=%fused_computation | loop fusion | flops 32 | bytes 256 | tf_op jit(solution)/shard_map/convert_element_type | solution.py:646
  96.0 0.7 select_reduce_fusion.source_ref
  96.7 7.3 %shard_map.123 = (bf16[16,48,512]{2,1,0:T(8,128)(2,1)}, f32[256,128]{1,0:T(8,128)}) custom-call(s32[16]{0:T(128)} %select_reduce_fusion.source_ref, f32[128]{0:T(128)} %gain_ref.1, bf16[32,13,16,128]{3,2,1,0:T(8,128)(2,1)} %get-tuple-element.8.got_ref, f32[32,8,128]{2,1,0:T(8,128)} %get-tuple-element.7.note_ref, f32[256,128]{1,0:T(8,128)} %get-tuple-element.9.dw_in_ref), custom_call_target="tpu_custom_call" | custom-call | flops 100000000 | bytes 4000000 | tf_op jit(solution)/shard_map/pallas_call | solution.py:618
  (1 shorter events, 0.0 us)

commit v3 on v2

--- a/solution.py
+++ b/solution.py
@@ -1,4 +1,5 @@
 import functools
+import math
 
 import jax
 import jax.numpy as jnp
@@ -20,6 +21,8 @@
 PAIR = 2 * BLK
 TILES = 13
 FAR = -1e30
+FAR_ENDS = (6, 8, 14, 16)
+NEAR_ENDS = (6, 8, 12, 15)
 
 
 class Grid:
@@ -228,10 +231,10 @@
     got_ref, notes_ref, dw_ref,
     xg_ref, wo_ref, full_ref, part_ref, rs_ref, give_ref, take_ref,
     x_ref, go_ref, b_ref, c_ref, send_ref, pre_ref, segs_ref, score_ref, score_t_ref, tile_ref, level_ref, note_ref,
-    gps_ref, half_ref, swap_ref, msg_ref, all_ref, heads_ref, xt_ref, d_ref, e1_ref, a1_ref, e2_ref, a2_ref, e3_ref,
+    gps_ref, half_ref, swap_ref, msg_ref, all_ref, heads_ref, xt_ref, d_ref, e1_ref, a1_ref, e2_ref,
     local_sem, load_sem, vs_sem, vr_sem, ts_sem, tr_sem, ps_sem, pr_sem, ss_sem, sr_sem,
-    es_sem, er_sem, ns_sem, nr_sem, ws_sem, wr_sem, gs_sem, gr_sem, cs_sem, cr_sem, xs_sem, xr_sem, ys_sem, yr_sem,
-    fs_sem, fr_sem, hs_sem, hr_sem, ks_sem, kr_sem, own_sem,
+    es_sem, er_sem, ns_sem, nr_sem, ws_sem, wr_sem, gs_sem, gr_sem, cs_sem, cr_sem, xs_sem, xr_sem,
+    hs_sem, hr_sem, ks_sem, kr_sem, own_sem,
 ):
     n_z, n_x, n_y, n_dp = grid.n_z, grid.n_x, grid.n_y, grid.n_dp
     dp, yy, xx, core, yh, z = grid.here()
@@ -245,18 +248,17 @@
     def at_z(step):
         return {"shard": yh * n_z + (z + step) % n_z}
 
-    def at_x(step):
-        return {"dp": grid.dp_of(yy, (xx + step) % n_x, core)}
-
-    def at_y(side, step):
-        place = grid.dp_of((yy + step) % n_y, xx, core)
+    def at_xy(side, step_x, step_y):
+        place = grid.dp_of((yy + step_y) % n_y, (xx + step_x) % n_x, core)
         return {"dp": place, "shard": shard if side == 0 else other}
+
+    plane = [(step_x, step_y) for step_x in range(n_x) for step_y in range(n_y)]
 
     barrier = pltpu.get_barrier_semaphore()
     for step in range(1, n_z):
         pl.semaphore_signal(barrier, inc=1, device_id=at_z(step), device_id_type=MESH)
-    for step in range(n_y):
-        pl.semaphore_signal(barrier, inc=1, device_id=at_y(1, step), device_id_type=MESH)
+    for step_x, step_y in plane:
+        pl.semaphore_signal(barrier, inc=1, device_id=at_xy(1, step_x, step_y), device_id_type=MESH)
 
     @pl.loop(0, n_dp - 1)
     def _(s):
@@ -279,7 +281,7 @@
         loads.append(pltpu.make_async_copy(feature_columns(side, 0), xg_ref.at[side, mine], local_sem.at[side]))
     for copy in loads:
         copy.start()
-    pl.semaphore_wait(barrier, n_dp - 1 + n_z - 1 + n_y)
+    pl.semaphore_wait(barrier, n_dp - 1 + n_z - 1 + n_x * n_y)
 
     weight_swap = remote(w_ref, wo_ref, vs_sem, vr_sem, across)
     weight_swap.start()
@@ -295,7 +297,10 @@
 
     for copy in loads[:3]:
         copy.wait()
-    marks = jnp.broadcast_to(starts_ref[...].astype(F32), (8, n_block * BLK))
+    rows = starts_ref[...].astype(F32)
+    marks = jnp.concatenate(
+        [jnp.broadcast_to(rows[r : r + 1], (8, rows.shape[1])) for r in range(rows.shape[0])], axis=1
+    )
     for q in range(n_block // 2):
         segs_ref[q] = spread_lanes(marks, q * PAIR)
 
@@ -333,9 +338,16 @@
                 send_ref[s, 4 * r + t] = whole[16 * r : 16 * r + 16, t * LANES : (t + 1) * LANES]
         send_ref[s, TILES - 1] = tile_ref[block]
 
-        @pl.when(s < n_dp - 1)
-        def _():
-            outgoing(s).start()
+    n_far = n_dp // 2
+
+    def batch(index):
+        for low, count, ends in ((0, n_far, FAR_ENDS), (n_far, n_dp - 1 - n_far, NEAR_ENDS)):
+            begin = low + (ends[index - 1] * count // ends[-1] if index else 0)
+            end = low + ends[index] * count // ends[-1]
+            if end > begin:
+                @pl.loop(begin, end)
+                def _(s):
+                    outgoing(s).start()
 
     own = pltpu.make_async_copy(send_ref.at[n_dp - 1], got_ref.at[n_dp - 1], own_sem.at[0])
     own.start()
@@ -344,6 +356,7 @@
     for copy in loads[3:]:
         copy.wait()
     weight_swap.wait()
+    batch(0)
     w_other = wo_ref[...].astype(F32).T.astype(BF16)
     for copy in token_copies:
         copy.wait()
@@ -375,35 +388,43 @@
     bias = per_head(bias_ref, shard * 8)
     lane = lanes()
 
-    def work(q):
-        grad_pre, level, step = mixer_pair(
-            pre_ref[q], score_ref[q], score_t_ref[q], rate, bias,
-            lambda duo: both(x_ref, q, duo * LANES), lambda duo: both(go_ref, q, duo * LANES),
-        )
-        gps_ref[q] = grad_pre
-        level_ref[2 * q] = jnp.where(lane < BLK, level, pltpu.roll(step, BLK, 1))
-        level_ref[2 * q + 1] = jnp.where(lane < BLK, pltpu.roll(level, LANES - BLK, 1), step)
-
-    @pl.loop(0, per_half // 2)
-    def _(q):
-        work(yh * per_half + q)
-
+    def work(*pairs):
+        done = [
+            mixer_pair(
+                pre_ref[q], score_ref[q], score_t_ref[q], rate, bias,
+                lambda duo, q=q: both(x_ref, q, duo * LANES), lambda duo, q=q: both(go_ref, q, duo * LANES),
+            )
+            for q in pairs
+        ]
+        for q, (grad_pre, level, step) in zip(pairs, done):
+            gps_ref[q] = grad_pre
+            level_ref[2 * q] = jnp.where(lane < BLK, level, pltpu.roll(step, BLK, 1))
+            level_ref[2 * q + 1] = jnp.where(lane < BLK, pltpu.roll(level, LANES - BLK, 1), step)
+
+    def work_span(low, count):
+        if count % 2:
+            @pl.loop(0, count)
+            def _(q):
+                work(low + q)
+        elif count:
+            @pl.loop(0, count // 2)
+            def _(q):
+                work(low + 2 * q, low + 2 * q + 1)
+
+    work_span(yh * per_half, per_half // 2)
     logit_swap.wait()
     others = take_ref[...]
     for q in range(per_half):
         pre_ref[(1 - yh) * per_half + q] = spread_lanes(others, q * PAIR)
 
-    @pl.loop(0, per_half)
-    def _(q):
-        work((1 - yh) * per_half + q)
+    batch(1)
+    work_span((1 - yh) * per_half, per_half)
 
     half_ref[0] = gather_lanes([gps_ref[(1 - yh) * per_half + i] for i in range(per_half)])
     grad_swap = remote(half_ref.at[0], swap_ref, ws_sem, wr_sem, across)
     grad_swap.start()
 
-    @pl.loop(per_half // 2, per_half)
-    def _(q):
-        work(yh * per_half + q)
+    work_span(yh * per_half + per_half // 2, per_half - per_half // 2)
 
     mine_half = gather_lanes([gps_ref[yh * per_half + i] for i in range(per_half)])
     grad_swap.wait()
@@ -413,6 +434,8 @@
         copy = remote(msg_ref, all_ref.at[step], gs_sem.at[step], gr_sem.at[step], at_z(step))
         copy.start()
         copies.append(copy)
+
+    batch(2)
 
     @pl.loop(0, n_dp)
     def _(s):
@@ -440,57 +463,43 @@
         product = lax.dot_general(xt_ref[side], grad_heads, NT, preferred_element_type=F32)
         for c in range(2):
             for x in range(n_x):
-                low = (c * n_x + x) * piece
-                d_ref[c, x, side] = product[low : low + piece]
+                for y in range(n_y):
+                    low = ((c * n_x + x) * n_y + y) * unit
+                    d_ref[c, x, y, side] = product[low : low + unit]
     copy = remote(d_ref.at[1 - core], e1_ref, cs_sem, cr_sem, sibling)
     copy.start()
     copy.wait()
     a1_ref[...] = d_ref[core] + e1_ref[...]
     copies = []
-    for step in range(1, n_x):
-        copy = remote(a1_ref.at[(xx + step) % n_x], e2_ref.at[step], xs_sem.at[step], xr_sem.at[step], at_x(step))
+    for step_x, step_y in plane[::-1]:
+        for side in (1, 0):
+            if side or step_x or step_y:
+                copy = remote(
+                    a1_ref.at[(xx + step_x) % n_x, (yy + step_y) % n_y, side], e2_ref.at[step_x, step_y, side],
+                    xs_sem.at[step_x, step_y, side], xr_sem.at[step_x, step_y, side], at_xy(side, step_x, step_y),
+                )
+                copy.start()
+                copies.append((step_x, step_y, side, copy))
+    total = a1_ref[xx, yy, 0]
+    for step_x, step_y, side, copy in copies:
+        copy.wait()
+        total = total + e2_ref[step_x, step_y, side]
+    side_rows = n_x * piece
+    low = pl.multiple_of(core * side_rows, side_rows)
+    mine = pl.ds(pl.multiple_of(low + (xx * n_y + yy) * unit, unit), unit)
+    dw_ref[mine] = total * (float(n_dp * n_block * BLK) ** -0.5)
+    copies = []
+    for step_x, step_y in plane[:0:-1]:
+        copy = remote(
+            dw_ref.at[mine], dw_ref.at[mine], hs_sem.at[step_x, step_y], hr_sem.at[step_x, step_y],
+            at_xy(0, step_x, step_y),
+        )
         copy.start()
         copies.append(copy)
-    total = a1_ref[xx]
-    for step, copy in enumerate(copies, 1):
-        copy.wait()
-        total = total + e2_ref[step]
-    a2_ref[...] = total
-    copies = []
-    for side in range(2):
-        for step in range(n_y):
-            if side or step:
-                rows = pl.ds(pl.multiple_of(((yy + step) % n_y) * unit, unit), unit)
-                copy = remote(
-                    a2_ref.at[side, rows], e3_ref.at[side, step],
-                    ys_sem.at[side, step], yr_sem.at[side, step], at_y(side, step),
-                )
-                copy.start()
-                copies.append((side, step, copy))
-    total = a2_ref[0, pl.ds(pl.multiple_of(yy * unit, unit), unit)]
-    for side, step, copy in copies:
-        copy.wait()
-        total = total + e3_ref[side, step]
-    low = pl.multiple_of((core * n_x + xx) * piece, piece)
-    mine = pl.ds(pl.multiple_of(low + yy * unit, unit), unit)
-    dw_ref[mine] = total * (float(n_dp * n_block * BLK) ** -0.5)
-    copies = []
-    for step in range(1, n_y):
-        copy = remote(dw_ref.at[mine], dw_ref.at[mine], fs_sem.at[step], fr_sem.at[step], at_y(0, step))
-        copy.start()
-        copies.append(copy)
+    batch(3)
     for copy in copies:
         copy.wait()
-    mine = pl.ds(low, piece)
-    copies = []
-    for step in range(1, n_x):
-        copy = remote(dw_ref.at[mine], dw_ref.at[mine], hs_sem.at[step], hr_sem.at[step], at_x(step))
-        copy.start()
-        copies.append(copy)
-    for copy in copies:
-        copy.wait()
-    side_rows = n_x * piece
-    mine = pl.ds(pl.multiple_of(core * side_rows, side_rows), side_rows)
+    mine = pl.ds(low, side_rows)
     copy = remote(dw_ref.at[mine], dw_ref.at[mine], ks_sem, kr_sem, sibling)
     copy.start()
     copy.wait()
@@ -510,7 +519,6 @@
     half = n_z * BLK
     feats, heads = weight.shape
     unit = feats // n_dp
-    piece = n_y * unit
     n_pair = n_block // 2
     dma = pltpu.SemaphoreType.DMA
     vmem = pl.BlockSpec(memory_space=pltpu.VMEM)
@@ -552,16 +560,13 @@
             pltpu.VMEM((n_z, 16, half), BF16),
             pltpu.VMEM((2, n_z, 8, half), F32),
             pltpu.VMEM((2, feats, half), BF16),
-            pltpu.VMEM((2, n_x, 2, piece, heads), F32),
-            pltpu.VMEM((n_x, 2, piece, heads), F32),
-            pltpu.VMEM((n_x, 2, piece, heads), F32),
-            pltpu.VMEM((n_x, 2, piece, heads), F32),
-            pltpu.VMEM((2, piece, heads), F32),
-            pltpu.VMEM((2, n_y, unit, heads), F32),
+            pltpu.VMEM((2, n_x, n_y, 2, unit, heads), F32),
+            pltpu.VMEM((n_x, n_y, 2, unit, heads), F32),
+            pltpu.VMEM((n_x, n_y, 2, unit, heads), F32),
+            pltpu.VMEM((n_x, n_y, 2, unit, heads), F32),
             dma((2,)), dma((4,)), dma, dma, dma((n_z, 2)), dma((n_z, 2)), dma((n_z,)), dma((n_z,)), dma, dma,
             dma((n_dp,)), dma((n_dp,)), dma((n_dp,)), dma((n_dp,)), dma, dma, dma((n_z,)), dma((n_z,)), dma, dma,
-            dma((n_x,)), dma((n_x,)), dma((2, n_y)), dma((2, n_y)), dma((n_y,)), dma((n_y,)),
-            dma((n_x,)), dma((n_x,)), dma, dma, dma((2,)),
+            dma((n_x, n_y, 2)), dma((n_x, n_y, 2)), dma((n_x, n_y)), dma((n_x, n_y)), dma, dma, dma((2,)),
         ],
         compiler_params=pltpu.CompilerParams(
             collective_id=0, has_side_effects=True, vmem_limit_bytes=60 * 1024 * 1024
@@ -570,19 +575,23 @@
     )(tokens, weight, x, go, b, c, starts, plan, bias, rate)
 
 
-def finish_kernel(source_ref, gain_ref, got_ref, note_ref, dw_in_ref, out_ref, dw_ref):
+def finish_kernel(gain_ref, got_ref, note_ref, dw_in_ref, out_ref, dw_ref, source_ref):
     shard = lax.axis_index("shard")
     lane = lanes()
+    n_slot, n_block = got_ref.shape[0], out_ref.shape[0]
+    labels = note_ref[:, 0, :]
+    slot = lax.broadcasted_iota(jnp.int32, labels.shape, 0).astype(F32)
+    labels = jnp.where(lax.broadcasted_iota(jnp.int32, labels.shape, 1) == LANES - 1, labels, 0.0)
+    for block in range(n_block):
+        found = jnp.sum(jnp.where(labels == float(block + 1), slot, 0.0))
+        source_ref[block] = jnp.clip(found.astype(jnp.int32), 0, n_slot - 1)
     dw_ref[...] = dw_in_ref[...]
     away_t = causal(True)
     pad = jnp.zeros((LANES - PAIR, LANES), BF16)
     low_half = lax.broadcasted_iota(jnp.int32, (PAIR, LANES), 1) < 64
 
-    @pl.loop(0, out_ref.shape[0] // 2)
-    def _(q):
-        last = got_ref.shape[0] - 1
-        first = jnp.clip(source_ref[2 * q], 0, last)
-        second = jnp.clip(source_ref[2 * q + 1], 0, last)
+    def formed(q):
+        first, second = source_ref[2 * q], source_ref[2 * q + 1]
         one, two = note_ref[first], note_ref[second]
         level = jnp.where(lane < BLK, one, jnp.where(lane < PAIR, pltpu.roll(two, BLK, 1), 0.0))
         step = jnp.where(lane < BLK, pltpu.roll(one, LANES - BLK, 1), jnp.where(lane < PAIR, two, 0.0))
@@ -590,6 +599,7 @@
         score_t = unpack_scores(
             got_ref[first, TILES - 1].astype(F32), got_ref[second, TILES - 1].astype(F32)
         )
+        grads = []
         for duo in range(4):
             mix_t = []
             for head in (2 * duo, 2 * duo + 1):
@@ -607,12 +617,22 @@
             )
             gv = jnp.where(low_half, gv[:PAIR], gv[PAIR:])
             gain = jnp.where(low_half, gain_ref[shard * 8 + 2 * duo], gain_ref[shard * 8 + 2 * duo + 1])
-            grad = (gv + gain * go.astype(F32)).astype(BF16)
-            out_ref[2 * q, :, duo * LANES : (duo + 1) * LANES] = grad[:BLK]
-            out_ref[2 * q + 1, :, duo * LANES : (duo + 1) * LANES] = grad[BLK:]
-
-
-def finish(sources, gain, got, notes, dw, n_block):
+            grads.append((gv + gain * go.astype(F32)).astype(BF16))
+        return grads
+
+    width = 2 if n_block % 4 == 0 else 1
+
+    @pl.loop(0, n_block // 2 // width)
+    def _(k):
+        pairs = [width * k + i for i in range(width)]
+        done = [formed(q) for q in pairs]
+        for q, grads in zip(pairs, done):
+            for duo, grad in enumerate(grads):
+                out_ref[2 * q, :, duo * LANES : (duo + 1) * LANES] = grad[:BLK]
+                out_ref[2 * q + 1, :, duo * LANES : (duo + 1) * LANES] = grad[BLK:]
+
+
+def finish(gain, got, notes, dw, n_block):
     vmem = pl.BlockSpec(memory_space=pltpu.VMEM)
     smem = pl.BlockSpec(memory_space=pltpu.SMEM)
     return pl.pallas_call(
@@ -621,11 +641,12 @@
             jax.ShapeDtypeStruct((n_block, BLK, 4 * LANES), BF16),
             jax.ShapeDtypeStruct(dw.shape, F32),
         ),
-        in_specs=[smem, smem, vmem, vmem, vmem],
+        in_specs=[smem, vmem, vmem, vmem],
         out_specs=[vmem, vmem],
+        scratch_shapes=[pltpu.SMEM((n_block,), jnp.int32)],
         compiler_params=pltpu.CompilerParams(vmem_limit_bytes=60 * 1024 * 1024),
         cost_estimate=pl.CostEstimate(flops=10**8, bytes_accessed=4 * 10**6, transcendentals=10**6),
-    )(sources, gain, got, notes, dw)
+    )(gain, got, notes, dw)
 
 
 def on_device(
@@ -641,13 +662,9 @@
 
     got, notes, dw = main_call(
         grid, residual_in, dt_weight, blocked(conv_out), blocked(grad_out), blocked(b_proj), blocked(c_proj),
-        doc_starts.reshape(1, rows), dest_plan, dt_bias, decay_rate,
-    )
-    labels = notes[:, 0, LANES - 1].astype(jnp.int32)
-    slots = jnp.arange(n_data, dtype=jnp.int32)
-    wanted = jnp.arange(1, n_block + 1, dtype=jnp.int32)
-    sources = jnp.sum(jnp.where(labels[None, :] == wanted[:, None], slots[None, :], 0), axis=1)
-    conv_grad, dw = finish(sources, skip_gain, got, notes, dw, n_block)
+        doc_starts.reshape(-1, math.gcd(rows, LANES)), dest_plan, dt_bias, decay_rate,
+    )
+    conv_grad, dw = finish(skip_gain, got, notes, dw, n_block)
     return conv_grad.reshape(rows, -1), dw
 
 

time: 104 us -> 86.9 us (0.84)
  Pallas kernels: 99.7 us -> 86.1 us
  other arithmetic: 2.37 us -> 0 us
  local copies, waits for them, and re-layouts: 1.27 us -> 0 us
    pallas_call x1, Pallas kernels: 92.4 us -> 79.5 us  [main_call(): pl.pallas_call(functools.partial(main_kernel, grid, n_block), out_shape=(...]
    convert_element_type x1 -> x0, other arithmetic: 1.64 us -> none  [on_device(): labels = notes[:, 0, LANES - 1].astype(jnp.int32)]
    reshape x1 -> x0, local copies, waits for them, and re-layouts: 1.27 us -> none  [on_device(): doc_starts.reshape(1, rows)]
where the time goes in v3:
time: 86.9 us; the launch traced here: 86.7 us
  Pallas kernels  86.1 us (99%)
    pallas_call x1, Pallas kernels, main_call(): pl.pallas_call(functools.partial(main_kernel, grid, n_block), out_shape=(...  79.5 us
    pallas_call x1, Pallas kernels, finish(): pl.pallas_call(finish_kernel, out_shape=(jax.ShapeDtypeStruct((n_block, B...  6.59 us

profile of v3, /device:TPU:1, one launch (start us, length us, event | category | flops | bytes accessed | tf_op | source)
XLA Modules:
  0.0 86.7 jit_solution(7537159433795157424)
XLA Ops:
  0.6 79.5 %shard_map.122 = (bf16[32,13,16,128]{3,2,1,0:T(8,128)(2,1)}, f32[32,8,128]{2,1,0:T(8,128)}, f32[256,128]{1,0:T(8,128)}) custom-call(bf16[48,4096]{1,0:T(8,128)(2,1)} %tokens_any.1, bf16[256,128]{1,0:T(8,128)(2,1)} %w_ref.1, bf16[16,48,512]{2,1,0:T(8,128)(2,1)} %bitcast.6, bf16[16,48,512]{2,1,0:T(8,128)(2,1)} %bitcast.7, bf16[16,48,512]{2,1,0:T(8,128)(2,1)} %bitcast.8, ...), custom_call_target="tpu_custom_call" | custom-call | flops 1000000000 | bytes 10000000 | tf_op jit(solution)/shard_map/pallas_call | solution.py:527
  80.1 6.6 %shard_map.123 = (bf16[16,48,512]{2,1,0:T(8,128)(2,1)}, f32[256,128]{1,0:T(8,128)}) custom-call(f32[128]{0:T(128)} %gain_ref.1, bf16[32,13,16,128]{3,2,1,0:T(8,128)(2,1)} %get-tuple-element.7.got_ref, f32[32,8,128]{2,1,0:T(8,128)} %get-tuple-element.8.note_ref, f32[256,128]{1,0:T(8,128)} %get-tuple-element.9.dw_in_ref), custom_call_target="tpu_custom_call" | custom-call | flops 100000000 | bytes 4000000 | tf_op jit(solution)/shard_map/pallas_call | solution.py:638

commit v4 on v3

--- a/solution.py
+++ b/solution.py
@@ -21,8 +21,8 @@
 PAIR = 2 * BLK
 TILES = 13
 FAR = -1e30
-FAR_ENDS = (6, 8, 14, 16)
-NEAR_ENDS = (6, 8, 12, 15)
+FAR_ENDS = (8, 9, 14, 16)
+NEAR_ENDS = (6, 8, 14, 15)
 
 
 class Grid:
@@ -127,14 +127,6 @@
     return lax.dot_general(a, b, NN, preferred_element_type=F32, precision=lax.Precision.HIGHEST)
 
 
-def split_dot(a, b):
-    high = b.astype(BF16)
-    low = (b - high.astype(F32)).astype(BF16)
-    return lax.dot_general(a, high, NT, preferred_element_type=F32) + lax.dot_general(
-        a, low, NT, preferred_element_type=F32
-    )
-
-
 def columns_of(*rows):
     filled = LANES - 8 * len(rows)
     return jnp.concatenate(list(rows) + [jnp.zeros((filled, LANES), F32)], axis=0).T
@@ -174,47 +166,49 @@
     )
 
 
-def mixer_pair(pre, score, score_t, rate, bias, x_of, go_of):
+def product_pair(score, score_t, x_of, go_of):
+    pad = jnp.zeros((LANES - PAIR, LANES), BF16)
+    low_half = lax.broadcasted_iota(jnp.int32, (PAIR, LANES), 1) < 64
+
+    def halves(rows):
+        zero = jnp.zeros_like(rows)
+        return jnp.concatenate([jnp.where(low_half, rows, zero), jnp.where(low_half, zero, rows)], axis=0)
+
+    by_i, by_j = [], []
+    for duo in range(4):
+        x, go = x_of(duo), go_of(duo)
+        wide = lax.dot_general(halves(go), jnp.concatenate([x, pad], axis=0), NT, preferred_element_type=F32)
+        wide_t = lax.dot_general(halves(x), jnp.concatenate([go, pad], axis=0), NT, preferred_element_type=F32)
+        for part in range(2):
+            by_i.append(wide[part * PAIR : (part + 1) * PAIR] * score)
+            by_j.append(wide_t[part * PAIR : (part + 1) * PAIR] * score_t)
+    return by_i, by_j
+
+
+def mixer_pair(pre, by_i, by_j, rate, bias):
     lane = lanes()
+    row = lax.broadcasted_iota(jnp.int32, (8, LANES), 0)
     gate = jnp.where(lane < PAIR, pre + bias, 0.0)
     e = jnp.exp(-jnp.abs(gate))
     series = e * (1.0 - e * (0.5 - e * (1.0 / 3.0 - e * (0.25 - e * 0.2))))
     log1p = jnp.where(e < 0.02, series, jnp.log(1.0 + e))
     step = jnp.maximum(gate, 0.0) + log1p
     sig = jnp.where(gate >= 0, 1.0, e) / (1.0 + e)
-    ratio = jnp.where((gate < 0) & (e < 1e-6), 1.0, sig / jnp.maximum(step, 1e-20))
     level = exact_dot(jnp.where(lane < PAIR, -step * rate, 0.0), triangle("ahead"))
     cols = columns_of(level, step)
     away, away_t = causal(False), causal(True)
-    pad = jnp.zeros((LANES - PAIR, LANES), BF16)
-    low_half = lax.broadcasted_iota(jnp.int32, (PAIR, LANES), 1) < 64
-    by_value, by_grad = [], []
-    for duo in range(4):
-        mix, mix_t = [], []
-        for head in (2 * duo, 2 * duo + 1):
-            level_col = cols[:PAIR, head : head + 1]
-            step_col = cols[:PAIR, 8 + head : 9 + head]
-            level_row = level[head : head + 1]
-            step_row = step[head : head + 1]
-            mix.append((score * jnp.exp(level_col - level_row + away) * step_row).astype(BF16))
-            mix_t.append((score_t * jnp.exp(level_row - level_col + away_t) * step_col).astype(BF16))
-        x = x_of(duo)
-        go = go_of(duo)
-        y = lax.dot_general(
-            jnp.concatenate(mix, axis=0), jnp.concatenate([x, pad], axis=0), NN, preferred_element_type=F32
-        )
-        gv = lax.dot_general(
-            jnp.concatenate(mix_t, axis=0), jnp.concatenate([go, pad], axis=0), NN, preferred_element_type=F32
-        )
-        by_value.append(x.astype(F32) * jnp.where(low_half, gv[:PAIR], gv[PAIR:]))
-        by_grad.append(go.astype(F32) * jnp.where(low_half, y[:PAIR], y[PAIR:]))
-    zeros = jnp.zeros((LANES - PAIR, 4 * LANES), F32)
-    head_of = lax.broadcasted_iota(jnp.int32, (8, 4 * LANES), 1) // 64
-    pick = jnp.where(head_of == lax.broadcasted_iota(jnp.int32, (8, 4 * LANES), 0), 1.0, 0.0).astype(BF16)
-    inflow = split_dot(pick, jnp.concatenate([jnp.concatenate(by_value, axis=1), zeros], axis=0))
-    outflow = split_dot(pick, jnp.concatenate([jnp.concatenate(by_grad, axis=1), zeros], axis=0))
-    grad_log = exact_dot(outflow - inflow, triangle("behind"))
-    return inflow * ratio - rate * grad_log * sig, level, step
+    grad_step = jnp.zeros((8, LANES), F32)
+    outflow = jnp.zeros((8, LANES), F32)
+    for head in range(8):
+        level_col = cols[:PAIR, head : head + 1]
+        step_col = cols[:PAIR, 8 + head : 9 + head]
+        level_row = level[head : head + 1]
+        weighted = by_i(head) * jnp.exp(level_col - level_row + away)
+        flow = by_j(head) * jnp.exp(level_row - level_col + away_t) * step_col
+        grad_step = jnp.where(row == head, jnp.sum(weighted, axis=0, keepdims=True), grad_step)
+        outflow = jnp.where(row == head, jnp.sum(flow, axis=0, keepdims=True), outflow)
+    grad_log = exact_dot(outflow - grad_step * step, triangle("behind"))
+    return (grad_step - rate * grad_log) * sig, level, step
 
 
 def per_head(ref, first_head):
@@ -229,11 +223,11 @@
     grid, n_block,
     tokens_any, w_ref, x_any, go_any, b_any, c_any, starts_ref, plan_ref, bias_ref, rate_ref,
     got_ref, notes_ref, dw_ref,
-    xg_ref, wo_ref, full_ref, part_ref, rs_ref, give_ref, take_ref,
+    stage_ref, xg_ref, wo_ref, full_ref, part_ref, rs_ref, give_ref, take_ref,
     x_ref, go_ref, b_ref, c_ref, send_ref, pre_ref, segs_ref, score_ref, score_t_ref, tile_ref, level_ref, note_ref,
-    gps_ref, half_ref, swap_ref, msg_ref, all_ref, heads_ref, xt_ref, d_ref, e1_ref, a1_ref, e2_ref,
+    by_i_ref, by_j_ref, label_ref, gps_ref, half_ref, swap_ref, msg_ref, all_ref, heads_ref, xt_ref, d_ref, e1_ref, a1_ref, e2_ref,
     local_sem, load_sem, vs_sem, vr_sem, ts_sem, tr_sem, ps_sem, pr_sem, ss_sem, sr_sem,
-    es_sem, er_sem, ns_sem, nr_sem, ws_sem, wr_sem, gs_sem, gr_sem, cs_sem, cr_sem, xs_sem, xr_sem,
+    es_sem, er_sem, qs_sem, qr_sem, ns_sem, nr_sem, ws_sem, wr_sem, gs_sem, gr_sem, cs_sem, cr_sem, xs_sem, xr_sem,
     hs_sem, hr_sem, ks_sem, kr_sem, own_sem,
 ):
     n_z, n_x, n_y, n_dp = grid.n_z, grid.n_x, grid.n_y, grid.n_dp
@@ -268,34 +262,96 @@
         owner = (yh if side == 0 else 1 - yh) * n_z + (z + step) % n_z
         return tokens_any.at[:, pl.ds(pl.multiple_of(owner * feats, feats), feats)]
 
-    mine = pl.ds(pl.multiple_of(z * BLK, BLK), BLK)
     group = (shard * 8) // (2 * n_z * 8 // G)
     cols = pl.ds(pl.multiple_of(group * N, N), N)
+    staged = []
+    for step in range(n_z):
+        for side in range(2):
+            target = stage_ref.at[step, side] if step else xg_ref.at[z, side]
+            staged.append(pltpu.make_async_copy(feature_columns(side, step), target, local_sem.at[step, side]))
+    for copy in staged:
+        copy.start()
     loads = [
         pltpu.make_async_copy(b_any.at[:, :, cols], b_ref, load_sem.at[2]),
         pltpu.make_async_copy(c_any.at[:, :, cols], c_ref, load_sem.at[3]),
         pltpu.make_async_copy(go_any, go_ref, load_sem.at[1]),
         pltpu.make_async_copy(x_any, x_ref, load_sem.at[0]),
     ]
-    for side in range(2):
-        loads.append(pltpu.make_async_copy(feature_columns(side, 0), xg_ref.at[side, mine], local_sem.at[side]))
     for copy in loads:
         copy.start()
     pl.semaphore_wait(barrier, n_dp - 1 + n_z - 1 + n_x * n_y)
 
-    weight_swap = remote(w_ref, wo_ref, vs_sem, vr_sem, across)
+    mirrored = {"dp": grid.dp_of(n_y - 1 - yy, xx, core), "shard": other}
+    weight_swap = remote(w_ref, wo_ref, vs_sem, vr_sem, mirrored)
     weight_swap.start()
+    for copy in staged:
+        copy.wait()
     token_copies = []
     for step in range(1, n_z):
-        for side in range(2):
-            copy = remote(
-                feature_columns(side, step), xg_ref.at[side, mine],
-                ts_sem.at[step, side], tr_sem.at[step, side], at_z(step),
-            )
-            copy.start()
-            token_copies.append(copy)
-
-    for copy in loads[:3]:
+        copy = remote(stage_ref.at[step], xg_ref.at[z], ts_sem.at[step], tr_sem.at[step], at_z(step))
+        copy.start()
+        token_copies.append(copy)
+
+    def label_of(s):
+        target = grid.partner(s)
+        label = jnp.int32(0)
+        for block in range(n_block):
+            label = label + jnp.where(plan_ref[block] == target, block + 1, 0)
+        return label
+
+    def outgoing(s):
+        body = pl.ds(0, TILES - 1)
+        return remote(
+            send_ref.at[s, body], got_ref.at[s, body], es_sem.at[s], er_sem.at[s], {"dp": grid.partner(s)}
+        )
+
+    def scored(s):
+        return remote(
+            send_ref.at[s, TILES - 1], got_ref.at[s, TILES - 1], qs_sem.at[s], qr_sem.at[s], {"dp": grid.partner(s)}
+        )
+
+    def noted(s):
+        return remote(note_ref.at[s], notes_ref.at[s], ns_sem.at[s], nr_sem.at[s], {"dp": grid.partner(s)})
+
+    def place(s):
+        label = label_of(s)
+        label_ref[s] = label
+        whole = go_ref[jnp.clip(label - 1, 0, n_block - 1)]
+        for r in range(3):
+            for t in range(4):
+                send_ref[s, 4 * r + t] = whole[16 * r : 16 * r + 16, t * LANES : (t + 1) * LANES]
+
+    n_far = n_dp // 2
+
+    def spans(index):
+        for low, count, ends in ((0, n_far, FAR_ENDS), (n_far, n_dp - 1 - n_far, NEAR_ENDS)):
+            begin = low + (ends[index - 1] * count // ends[-1] if index else 0)
+            end = low + ends[index] * count // ends[-1]
+            if end > begin:
+                yield begin, end
+
+    def batch(index):
+        for begin, end in spans(index):
+            @pl.loop(begin, end)
+            def _(s):
+                outgoing(s).start()
+
+    loads[2].wait()
+    for begin, end in spans(0):
+        @pl.loop(begin, end)
+        def _(s):
+            place(s)
+            outgoing(s).start()
+
+    for index in (1, 2, 3):
+        for begin, end in spans(index):
+            @pl.loop(begin, end)
+            def _(s):
+                place(s)
+
+    place(n_dp - 1)
+
+    for copy in loads[:2]:
         copy.wait()
     rows = starts_ref[...].astype(F32)
     marks = jnp.concatenate(
@@ -316,38 +372,9 @@
         tile_ref[2 * q] = one.astype(BF16)
         tile_ref[2 * q + 1] = two.astype(BF16)
 
-    def label_of(s):
-        target = grid.partner(s)
-        label = jnp.int32(0)
-        for block in range(n_block):
-            label = label + jnp.where(plan_ref[block] == target, block + 1, 0)
-        return label
-
-    def outgoing(s):
-        return remote(send_ref.at[s], got_ref.at[s], es_sem.at[s], er_sem.at[s], {"dp": grid.partner(s)})
-
-    def noted(s):
-        return remote(note_ref.at[s], notes_ref.at[s], ns_sem.at[s], nr_sem.at[s], {"dp": grid.partner(s)})
-
     @pl.loop(0, n_dp)
     def _(s):
-        block = jnp.clip(label_of(s) - 1, 0, n_block - 1)
-        whole = go_ref[block]
-        for r in range(3):
-            for t in range(4):
-                send_ref[s, 4 * r + t] = whole[16 * r : 16 * r + 16, t * LANES : (t + 1) * LANES]
-        send_ref[s, TILES - 1] = tile_ref[block]
-
-    n_far = n_dp // 2
-
-    def batch(index):
-        for low, count, ends in ((0, n_far, FAR_ENDS), (n_far, n_dp - 1 - n_far, NEAR_ENDS)):
-            begin = low + (ends[index - 1] * count // ends[-1] if index else 0)
-            end = low + ends[index] * count // ends[-1]
-            if end > begin:
-                @pl.loop(begin, end)
-                def _(s):
-                    outgoing(s).start()
+        send_ref[s, TILES - 1] = tile_ref[jnp.clip(label_ref[s] - 1, 0, n_block - 1)]
 
     own = pltpu.make_async_copy(send_ref.at[n_dp - 1], got_ref.at[n_dp - 1], own_sem.at[0])
     own.start()
@@ -355,13 +382,24 @@
     w_here = w_ref[...].astype(F32).T.astype(BF16)
     for copy in loads[3:]:
         copy.wait()
+
+    @pl.loop(0, n_block // 2)
+    def _(q):
+        by_i, by_j = product_pair(
+            score_ref[q], score_t_ref[q],
+            lambda duo: both(x_ref, q, duo * LANES), lambda duo: both(go_ref, q, duo * LANES),
+        )
+        for head in range(8):
+            by_i_ref[q, head] = by_i[head]
+            by_j_ref[q, head] = by_j[head]
+
     weight_swap.wait()
-    batch(0)
     w_other = wo_ref[...].astype(F32).T.astype(BF16)
     for copy in token_copies:
         copy.wait()
-    full_ref[...] = lax.dot_general(w_here, xg_ref[0], NT, preferred_element_type=F32) + lax.dot_general(
-        w_other, xg_ref[1], NT, preferred_element_type=F32
+    columns = [xg_ref[:, side].reshape(n_z * BLK, feats) for side in range(2)]
+    full_ref[...] = lax.dot_general(w_here, columns[0], NT, preferred_element_type=F32) + lax.dot_general(
+        w_other, columns[1], NT, preferred_element_type=F32
     )
     copies = []
     for step in list(range(1, n_z)) + [0]:
@@ -373,7 +411,7 @@
             copy.start()
             copies.append(copy)
     for side in range(2):
-        xt_ref[side] = xg_ref[side].astype(F32).T.astype(BF16)
+        xt_ref[side] = columns[side].astype(F32).T.astype(BF16)
     total = part_ref[0]
     for step, copy in enumerate(copies, 1):
         copy.wait()
@@ -391,8 +429,7 @@
     def work(*pairs):
         done = [
             mixer_pair(
-                pre_ref[q], score_ref[q], score_t_ref[q], rate, bias,
-                lambda duo, q=q: both(x_ref, q, duo * LANES), lambda duo, q=q: both(go_ref, q, duo * LANES),
+                pre_ref[q], lambda head, q=q: by_i_ref[q, head], lambda head, q=q: by_j_ref[q, head], rate, bias
             )
             for q in pairs
         ]
@@ -439,11 +476,12 @@
 
     @pl.loop(0, n_dp)
     def _(s):
-        label = label_of(s)
+        label = label_ref[s]
         note_ref[s] = jnp.where(lane < PAIR, level_ref[jnp.clip(label - 1, 0, n_block - 1)], label.astype(F32))
 
         @pl.when(s < n_dp - 1)
         def _():
+            scored(s).start()
             noted(s).start()
 
     own_note = pltpu.make_async_copy(note_ref.at[n_dp - 1], notes_ref.at[n_dp - 1], own_sem.at[1])
@@ -506,6 +544,7 @@
 
     @pl.loop(0, n_dp - 1)
     def _(s):
+        scored(s).wait()
         noted(s).wait()
         outgoing(s).wait()
 
@@ -534,7 +573,8 @@
         in_specs=[hbm, vmem, hbm, hbm, hbm, hbm, vmem, smem, smem, smem],
         out_specs=[hbm, hbm, vmem],
         scratch_shapes=[
-            pltpu.VMEM((2, half, feats), BF16),
+            pltpu.VMEM((n_z, 2, BLK, feats), BF16),
+            pltpu.VMEM((n_z, 2, BLK, feats), BF16),
             pltpu.VMEM((feats, heads), BF16),
             pltpu.VMEM((heads, half), F32),
             pltpu.VMEM((n_z, 16, half), F32),
@@ -553,6 +593,9 @@
             pltpu.VMEM((n_block, 16, LANES), BF16),
             pltpu.VMEM((n_block, 8, LANES), F32),
             pltpu.VMEM((n_dp, 8, LANES), F32),
+            pltpu.VMEM((n_pair, 8, PAIR, LANES), F32),
+            pltpu.VMEM((n_pair, 8, PAIR, LANES), F32),
+            pltpu.SMEM((n_dp,), jnp.int32),
             pltpu.VMEM((n_pair, 8, LANES), F32),
             pltpu.VMEM((1, 8, half), F32),
             pltpu.VMEM((8, half), F32),
@@ -564,8 +607,8 @@
             pltpu.VMEM((n_x, n_y, 2, unit, heads), F32),
             pltpu.VMEM((n_x, n_y, 2, unit, heads), F32),
             pltpu.VMEM((n_x, n_y, 2, unit, heads), F32),
-            dma((2,)), dma((4,)), dma, dma, dma((n_z, 2)), dma((n_z, 2)), dma((n_z,)), dma((n_z,)), dma, dma,
-            dma((n_dp,)), dma((n_dp,)), dma((n_dp,)), dma((n_dp,)), dma, dma, dma((n_z,)), dma((n_z,)), dma, dma,
+            dma((n_z, 2)), dma((4,)), dma, dma, dma((n_z,)), dma((n_z,)), dma((n_z,)), dma((n_z,)), dma, dma,
+            dma((n_dp,)), dma((n_dp,)), dma((n_dp,)), dma((n_dp,)), dma((n_dp,)), dma((n_dp,)), dma, dma, dma((n_z,)), dma((n_z,)), dma, dma,
             dma((n_x, n_y, 2)), dma((n_x, n_y, 2)), dma((n_x, n_y)), dma((n_x, n_y)), dma, dma, dma((2,)),
         ],
         compiler_params=pltpu.CompilerParams(

time: 86.9 us -> 84.3 us (0.970)
  Pallas kernels: 86.1 us -> 83.5 us
    pallas_call x1, Pallas kernels: 79.5 us -> 76.9 us  [main_call(): pl.pallas_call(functools.partial(main_kernel, grid, n_block), out_shape=(...]
where the time goes in v4:
time: 84.3 us; the launch traced here: 84.1 us
  Pallas kernels  83.5 us (99%)
    pallas_call x1, Pallas kernels, main_call(): pl.pallas_call(functools.partial(main_kernel, grid, n_block), out_shape=(...  76.9 us
    pallas_call x1, Pallas kernels, finish(): pl.pallas_call(finish_kernel, out_shape=(jax.ShapeDtypeStruct((n_block, B...  6.59 us

profile of v4, /device:TPU:1, one launch (start us, length us, event | category | flops | bytes accessed | tf_op | source)
XLA Modules:
  0.0 84.1 jit_solution(11749881611758746662)
XLA Ops:
  0.6 76.9 %shard_map.122 = (bf16[32,13,16,128]{3,2,1,0:T(8,128)(2,1)}, f32[32,8,128]{2,1,0:T(8,128)}, f32[256,128]{1,0:T(8,128)}) custom-call(bf16[48,4096]{1,0:T(8,128)(2,1)} %tokens_any.1, bf16[256,128]{1,0:T(8,128)(2,1)} %w_ref.1, bf16[16,48,512]{2,1,0:T(8,128)(2,1)} %bitcast.6, bf16[16,48,512]{2,1,0:T(8,128)(2,1)} %bitcast.7, bf16[16,48,512]{2,1,0:T(8,128)(2,1)} %bitcast.8, ...), custom_call_target="tpu_custom_call" | custom-call | flops 1000000000 | bytes 10000000 | tf_op jit(solution)/shard_map/pallas_call | solution.py:566
  77.5 6.6 %shard_map.123 = (bf16[16,48,512]{2,1,0:T(8,128)(2,1)}, f32[256,128]{1,0:T(8,128)}) custom-call(f32[128]{0:T(128)} %gain_ref.1, bf16[32,13,16,128]{3,2,1,0:T(8,128)(2,1)} %get-tuple-element.7.got_ref, f32[32,8,128]{2,1,0:T(8,128)} %get-tuple-element.8.note_ref, f32[256,128]{1,0:T(8,128)} %get-tuple-element.9.dw_in_ref), custom_call_target="tpu_custom_call" | custom-call | flops 100000000 | bytes 4000000 | tf_op jit(solution)/shard_map/pallas_call | solution.py:681

commit v5 on v4

--- a/solution.py
+++ b/solution.py
@@ -376,6 +376,10 @@
     def _(s):
         send_ref[s, TILES - 1] = tile_ref[jnp.clip(label_ref[s] - 1, 0, n_block - 1)]
 
+        @pl.when(s < n_dp - 1)
+        def _():
+            scored(s).start()
+
     own = pltpu.make_async_copy(send_ref.at[n_dp - 1], got_ref.at[n_dp - 1], own_sem.at[0])
     own.start()
 
@@ -481,7 +485,6 @@
 
         @pl.when(s < n_dp - 1)
         def _():
-            scored(s).start()
             noted(s).start()
 
     own_note = pltpu.make_async_copy(note_ref.at[n_dp - 1], notes_ref.at[n_dp - 1], own_sem.at[1])

time: 84.3 us -> 83.9 us (level)
  no operation moved by 1% of the time
where the time goes in v5:
time: 83.9 us; the launch traced here: 83.7 us
  Pallas kernels  83 us (99%)
    pallas_call x1, Pallas kernels, main_call(): pl.pallas_call(functools.partial(main_kernel, grid, n_block), out_shape=(...  76.5 us
    pallas_call x1, Pallas kernels, finish(): pl.pallas_call(finish_kernel, out_shape=(jax.ShapeDtypeStruct((n_block, B...  6.6 us

profile of v5, /device:TPU:1, one launch (start us, length us, event | category | flops | bytes accessed | tf_op | source)
XLA Modules:
  0.0 83.7 jit_solution(871358518337053268)
XLA Ops:
  0.6 76.5 %shard_map.122 = (bf16[32,13,16,128]{3,2,1,0:T(8,128)(2,1)}, f32[32,8,128]{2,1,0:T(8,128)}, f32[256,128]{1,0:T(8,128)}) custom-call(bf16[48,4096]{1,0:T(8,128)(2,1)} %tokens_any.1, bf16[256,128]{1,0:T(8,128)(2,1)} %w_ref.1, bf16[16,48,512]{2,1,0:T(8,128)(2,1)} %bitcast.6, bf16[16,48,512]{2,1,0:T(8,128)(2,1)} %bitcast.7, bf16[16,48,512]{2,1,0:T(8,128)(2,1)} %bitcast.8, ...), custom_call_target="tpu_custom_call" | custom-call | flops 1000000000 | bytes 10000000 | tf_op jit(solution)/shard_map/pallas_call | solution.py:569
  77.1 6.6 %shard_map.123 = (bf16[16,48,512]{2,1,0:T(8,128)(2,1)}, f32[256,128]{1,0:T(8,128)}) custom-call(f32[128]{0:T(128)} %gain_ref.1, bf16[32,13,16,128]{3,2,1,0:T(8,128)(2,1)} %get-tuple-element.7.got_ref, f32[32,8,128]{2,1,0:T(8,128)} %get-tuple-element.8.note_ref, f32[256,128]{1,0:T(8,128)} %get-tuple-element.9.dw_in_ref), custom_call_target="tpu_custom_call" | custom-call | flops 100000000 | bytes 4000000 | tf_op jit(solution)/shard_map/pallas_call | solution.py:684
